TPU v7x, 32 devices: a whole 2x2x4 slice. The times are simulated.
32 devices in a mesh: groups: 2 (over x), blk: 16 (over z, y, core).
Axes of the slice: x: 2, y: 2, z: 4, core: 2. Of those that a mesh axis runs over, the one named last changes fastest.
Arguments:
- records: bfloat16 [8192, 2048], P(('groups', 'blk')), parts along dimension 0, may hold values from -6 to 6
- dest: int32 [8192, 1], P(('groups', 'blk')), parts along dimension 0, may hold values from 0 to 15; in each aligned block of 256 rows (0 to 255, 256 to 511, ...) at most 32 rows name the same one
- slot: int32 [8192, 1], P(('groups', 'blk')), parts along dimension 0, may hold values from 0 to 255
- valid: int32 [8192, 1], P(('groups', 'blk')), parts along dimension 0, may hold values from 256 to 2048
- masks: int32 [2], replicated, may hold values from 1 to 15, as said below
Outputs:
- correlations: bfloat16 [2, 4096, 128, 128], P(None, ('groups', 'blk')), parts along dimension 1
There are 2 independent parts, one for each index of `groups`. A program takes and returns all parts, laid end to end along the dimension named above; an argument that names none is the same for every part. Nothing has to cross between parts.
Inputs may be any that keep to these rules, and one draw needn't show every extreme that they name: `dest`: in the rows of one device no block is named more than 32 times. `masks`: 2 distinct numbers; one of them is 15.
All inputs are finite; a program needn't handle non-finite values.
Results may differ from a plain program's by a relative error of at most 0.0085.
Values may be sent and summed in bfloat16 or wider, within the bound.
No kernel may reach another device: no remote copies, remote signals or barrier semaphores. Data moves between devices by JAX's collectives and lax.ppermute only.
A program may use at most 128 MiB of HBM per device.

v0:
```python
import functools
import math

import jax
import jax.numpy as jnp
import numpy as np
from jax import lax
from jax.experimental import pallas as pl
from jax.experimental.pallas import tpu as pltpu
from jax.sharding import PartitionSpec as P

CH = 128
F = 256
LAGS = 128
W = 2
LOW_BITS = 4


def bin_order(bins):
    return np.concatenate([np.arange(2, bins + 1, 2), np.arange(1, bins + 1, 2)])


def forward_table(nfft, bins):
    sample = np.arange(nfft // 2, dtype=np.int64)[:, None]
    angle = (sample * bin_order(bins)[None, :] % nfft) * (2.0 * math.pi / nfft)
    cos, sin = np.cos(angle), np.sin(angle)
    half = bins // 2
    table = [cos[:, :half], -sin[:, :half], cos[:, half:], -sin[:, half:]]
    return np.concatenate(table, axis=1).astype(np.float32).astype(jnp.bfloat16)


def lag_tables(nfft, bins, lags, scale):
    half = lags // 2
    count = lags + 1
    place = np.arange(count)
    middle = ((count - 1 - 2 * place) / 2.0) ** 2 * math.cos(2.0 * math.pi * bins / nfft)
    aside = (place[1:] * (count - place[1:])) / 2.0
    _, basis = np.linalg.eigh(np.diag(middle) + np.diag(aside, 1) + np.diag(aside, -1))
    basis = basis[:, ::-1][:, :half]
    even, odd = basis[:, 0::2], basis[:, 1::2]
    even = even * np.sign(even[half])
    odd = odd * np.sign(odd[half + 1])
    freq = bin_order(bins)[None, :]
    angle = (freq * (place[:, None] - half) % nfft) * (2.0 * math.pi / nfft)
    rows = [even.T @ np.cos(angle), odd.T @ -np.sin(angle)]
    rest = np.cos(angle) - np.sin(angle) - even @ rows[0] - odd @ rows[1]
    assert np.abs(rest).max() < 1e-7
    rows = np.concatenate(rows + [-rows[1]])
    basis = np.concatenate([even, odd], axis=1)[:lags].T * scale
    blank = np.zeros_like(basis)
    spread = np.concatenate(
        [np.concatenate([basis if k == n else blank for n in range(4)], axis=1) for k in range(4)]
    )

    def narrow(table):
        return (np.round(table * 2.0**28) / 2.0**28).astype(np.float32).astype(jnp.bfloat16)

    return narrow(rows), narrow(spread)


def iota(shape, dim):
    return lax.broadcasted_iota(jnp.int32, shape, dim)


LABELS = 8


def full_plan(capacity, chunks):
    return (capacity,) * chunks


def short_plan(capacity, chunks):
    eighths = (8, 8, 8, 8, 8, 8, 8, 8, 8, 7, 7, 6, 6, 5, 4, 3)
    return tuple(capacity * eighths[c * len(eighths) // chunks] // 8 for c in range(chunks))


def pack_kernel(
    owners, capacity, plans, me_ref, dest_hbm, slot_hbm, valid_hbm, records_hbm, *refs
):
    *out_refs, dest_ref, slot_ref, valid_ref, records_ref, sems = refs
    held, nfft = records_ref.shape
    rows = owners * capacity
    width = 512
    small = [
        pltpu.make_async_copy(source, target, sems.at[k])
        for k, (source, target) in enumerate(
            [(dest_hbm, dest_ref), (slot_hbm, slot_ref), (valid_hbm, valid_ref)]
        )
    ]
    large = [
        pltpu.make_async_copy(
            records_hbm.at[:, pl.ds(begin, width)],
            records_ref.at[:, pl.ds(begin, width)],
            sems.at[3 + begin // width],
        )
        for begin in range(0, nfft, width)
    ]
    for copy in small + large:
        copy.start()
    for copy in small:
        copy.wait()
    part = dest_ref[...]
    if len(out_refs) > 1:
        part = part ^ me_ref[0]
    valid = valid_ref[...]
    first = valid * held + (held - 1 - iota((1, held), 1))

    def column(row):
        wide = jnp.transpose(jnp.broadcast_to(row.astype(jnp.float32), (128, held)))
        return jnp.concatenate([wide] * (held // 128), axis=1)

    same = column(part) == part.astype(jnp.float32)
    before = jnp.where(same & (column(first) > first.astype(jnp.float32)), 1.0, 0.0)
    rank = jnp.sum(before, axis=0, keepdims=True).astype(jnp.int32)
    over = jnp.zeros((1, held), jnp.int32)
    for plan in sorted(set(plans)):
        member = functools.reduce(
            jnp.logical_or, [part == d for d in range(owners) if plans[d] == plan]
        )
        for size in sorted(set(plan)):
            if size < capacity:
                reach = 128 * sum(count > size for count in plan)
                over += jnp.where(member & (rank >= size) & (valid > reach), 1, 0)
    over = jnp.max(jnp.minimum(over, 1).astype(jnp.float32), axis=1, keepdims=True)
    position = part * capacity + rank
    order = (iota((rows, held), 0) == position).astype(jnp.float32).astype(jnp.bfloat16)
    row = iota((16, held), 0)
    labels = jnp.where(
        row == 0,
        slot_ref[...],
        jnp.where(
            row == 1,
            valid >> LOW_BITS,
            jnp.where(row == 2, valid & ((1 << LOW_BITS) - 1), 0),
        ),
    )
    moved = lax.dot_general(
        labels.astype(jnp.float32).astype(jnp.bfloat16),
        order,
        (((1,), (1,)), ((), ())),
        preferred_element_type=jnp.float32,
    )
    moved = jnp.where(iota((16, rows), 0) == 3, over, moved).astype(jnp.bfloat16)

    def put(d, at, value):
        if len(out_refs) > 1:
            out_refs[d][at : at + value.shape[0], :] = value
        else:
            out_refs[0][d, at : at + value.shape[0], :] = value

    for d in range(owners):
        at = d * capacity // 128 * 128
        put(d, sum(plans[d]), moved[:LABELS, at : at + 128])
    for begin in range(0, nfft, width):
        large[begin // width].wait()
        ordered = jnp.dot(
            order, records_ref[:, begin : begin + width], preferred_element_type=jnp.float32
        ).astype(jnp.bfloat16)
        for lane in range(0, width, 128):
            c = (begin + lane) // 128
            for d in range(owners):
                top = d * capacity
                put(d, sum(plans[d][:c]), ordered[top : top + plans[d][c], lane : lane + 128])


def pack(me, labels, records, capacity, plans, split):
    held, nfft = records.shape
    owners = len(plans)
    hbm = pl.BlockSpec(memory_space=pltpu.HBM)
    vmem = pl.BlockSpec(memory_space=pltpu.VMEM)
    shapes = [(sum(plan) + LABELS, 128) for plan in plans]
    if not split:
        shapes = [(owners,) + shapes[0]]
    return pl.pallas_call(
        functools.partial(pack_kernel, owners, capacity, plans),
        in_specs=[pl.BlockSpec(memory_space=pltpu.SMEM)] + [hbm] * 4,
        out_specs=[vmem] * len(shapes),
        out_shape=[jax.ShapeDtypeStruct(shape, jnp.bfloat16) for shape in shapes],
        scratch_shapes=[pltpu.VMEM((1, held), jnp.int32)] * 3
        + [pltpu.VMEM((held, nfft), jnp.bfloat16), pltpu.SemaphoreType.DMA((3 + nfft // 512,))],
        compiler_params=pltpu.CompilerParams(vmem_limit_bytes=48 * 1024 * 1024),
        name="pack",
    )(me, *labels, records)


def whiten_kernel(capacity, plans, places, me_ref, mask_ref, *refs):
    *arrived_refs, table_hbm, low_ref, high_ref, branch_ref, table_ref, trace_ref, spectrum_ref, sems = refs
    owners = len(plans)
    split = len(arrived_refs) > 1
    nfft = trace_ref.shape[1]
    rows = owners * capacity
    slots = CH * W
    bins = table_ref.shape[1] // 2
    shift = capacity.bit_length() - 1
    width = 256
    depth = 512
    loads = [
        pltpu.make_async_copy(
            table_hbm.at[pl.ds(at, depth)], table_ref.at[pl.ds(at, depth)], sems.at[at // depth]
        )
        for at in range(0, nfft // 2, depth)
    ]
    for copy in loads:
        copy.start()

    def take(c):
        if not split:
            at, count = sum(plans[0][:c]), plans[0][c] if c < len(plans[0]) else LABELS
            return arrived_refs[0][:, at : at + count, :].reshape(owners * count, 128)
        pieces = []
        for ref, plan in zip(arrived_refs, plans):
            at, count = sum(plan[:c]), plan[c] if c < len(plan) else LABELS
            pieces.append(ref[at : at + count, :])
            if c < len(plan) and count < capacity:
                pieces.append(jnp.zeros((capacity - count, 128), jnp.bfloat16))
        return jnp.concatenate(pieces, axis=0)

    labels = take(len(plans[0])).astype(jnp.float32).reshape(owners, LABELS, 128)
    which = iota((owners, LABELS, 128), 1)
    over = jnp.max(jnp.where(which == 3, labels, 0.0))
    branch_ref[0] = jnp.where(over > 0.0, owners - 2, mask_ref[0] - 1)
    parts = jnp.concatenate(
        [jnp.sum(jnp.where(which == k, labels, 0.0), axis=1) for k in range(3)], axis=0
    )
    if split:
        part = iota((1, rows), 1) >> shift
        place = functools.reduce(
            lambda total, p: total + jnp.where(part == p, places[p], 0),
            range(owners),
            jnp.zeros((1, rows), jnp.int32),
        )
    else:
        place = me_ref[0]
    base = (place * capacity) & 127
    pick = iota((128, rows), 0) == base + (iota((128, rows), 1) & (capacity - 1))
    picked = jnp.dot(
        parts.astype(jnp.bfloat16),
        pick.astype(jnp.float32).astype(jnp.bfloat16),
        preferred_element_type=jnp.float32,
    )
    source = iota((owners, rows), 0) == iota((owners, rows), 1) >> shift
    rowed = [
        jnp.sum(
            jnp.where(source, picked[k * owners : (k + 1) * owners], 0.0), axis=0, keepdims=True
        )
        for k in range(3)
    ]
    slot_row = rowed[0].astype(jnp.int32)
    place = (slot_row & (W - 1)) * CH + (slot_row >> (W.bit_length() - 1))
    valid_row = rowed[1] * float(1 << LOW_BITS) + rowed[2]
    scatter = (iota((slots, rows), 0) == place).astype(jnp.float32).astype(jnp.bfloat16)
    valid_col = jnp.transpose(jnp.broadcast_to(valid_row, (128, rows))).astype(jnp.int32)
    power = jnp.zeros((slots, 128), jnp.float32)
    for begin in range(0, nfft, width):
        lanes = range(begin, begin + width, 128)
        inside = jnp.concatenate(
            [
                (iota((rows, 128), 1) + lane < valid_col).astype(jnp.float32).astype(jnp.bfloat16)
                for lane in lanes
            ],
            axis=1,
        )
        arrived = jnp.concatenate([take(lane // 128) for lane in lanes], axis=1)
        summed = jnp.dot(scatter, arrived * inside, preferred_element_type=jnp.float32)
        coverage = jnp.dot(scatter, inside, preferred_element_type=jnp.float32)
        trace = summed / jnp.maximum(coverage, 1.0)
        trace_ref[:, begin : begin + width] = trace
        square = trace * trace
        for lane in range(0, width, 128):
            power = power + square[:, lane : lane + 128]
    meansq = jnp.sum(power, axis=1, keepdims=True) * (1.0 / nfft)
    gain = lax.rsqrt(meansq + 1e-06)
    for begin in range(0, nfft // 2, depth):
        loads[begin // depth].wait()
        near = trace_ref[:, begin : begin + depth] * gain
        far = trace_ref[:, begin + nfft // 2 : begin + nfft // 2 + depth] * gain
        for at, folded in ((0, near + far), (bins, near - far)):
            part = jnp.dot(
                folded.astype(jnp.bfloat16),
                table_ref[begin : begin + depth, at : at + bins],
                preferred_element_type=jnp.float32,
            )
            if begin == 0:
                spectrum_ref[:, at : at + bins] = part
            else:
                spectrum_ref[:, at : at + bins] += part
    half = bins // 2
    for at in (0, bins):
        real_part = spectrum_ref[:, at : at + half]
        imag_part = spectrum_ref[:, at + half : at + bins]
        amplitude = lax.rsqrt(
            jnp.maximum(real_part * real_part + imag_part * imag_part, nfft / 4.0)
        )
        for part, offset in ((real_part, 0), (imag_part, bins)):
            white = (part * amplitude).astype(jnp.bfloat16)
            for w in range(W):
                lane = w * 2 * bins + offset + at // 2
                top = w * CH
                low_ref[:, lane : lane + half] = white[top : top + CH // 2]
                high_ref[:, lane : lane + half] = white[top + CH // 2 : top + CH]


def whiten(me, mask, arrived, table, capacity, plans, places):
    nfft, width = 2 * table.shape[0], table.shape[1]
    vmem = pl.BlockSpec(memory_space=pltpu.VMEM)
    smem = pl.BlockSpec(memory_space=pltpu.SMEM)
    return pl.pallas_call(
        functools.partial(whiten_kernel, capacity, plans, places),
        in_specs=[smem, smem]
        + [vmem] * len(arrived)
        + [pl.BlockSpec(memory_space=pltpu.HBM)],
        out_specs=[vmem, vmem, smem],
        out_shape=[
            jax.ShapeDtypeStruct((CH // 2, W * width), jnp.bfloat16),
            jax.ShapeDtypeStruct((CH // 2, W * width), jnp.bfloat16),
            jax.ShapeDtypeStruct((1,), jnp.int32),
        ],
        scratch_shapes=[
            pltpu.VMEM(table.shape, jnp.bfloat16),
            pltpu.VMEM((CH * W, nfft), jnp.float32),
            pltpu.VMEM((CH * W, width), jnp.float32),
            pltpu.SemaphoreType.DMA((nfft // 1024,)),
        ],
        compiler_params=pltpu.CompilerParams(vmem_limit_bytes=50 * 1024 * 1024),
        name="whiten",
    )(me, mask, *arrived, table)


BLOCK = 32
PIECE = 16


def correlate_kernel(
    order_ref, own_low, own_high, rows_ref, spread_ref, *refs
):
    *partners, out_hbm, both_ref, wide_ref, near_ref, turned_a, turned_b, found_a, found_b, out_ref, sems, loaded = refs
    bins = rows_ref.shape[1]
    terms = rows_ref.shape[0] // 3
    lags = out_ref.shape[4]
    blocks = CH // BLOCK
    turned, found = (turned_a, turned_b), (found_a, found_b)

    def turn(block, slot):
        even = rows_ref[:terms, :]
        odd = rows_ref[terms : 2 * terms, :]
        minus = rows_ref[2 * terms :, :]
        for k in range(BLOCK):
            u = wide_ref[pl.ds(block * BLOCK + k, 1), :]
            top = slice(2 * k * terms, (2 * k + 1) * terms)
            low = slice((2 * k + 1) * terms, (2 * k + 2) * terms)
            for w in range(W):
                at = w * 2 * bins
                real, imag = slice(at, at + bins), slice(at + bins, at + 2 * bins)
                ur = jnp.broadcast_to(u[:, real], (terms, bins)).astype(jnp.bfloat16)
                ui = jnp.broadcast_to(u[:, imag], (terms, bins)).astype(jnp.bfloat16)
                turned[slot][top, real] = ur * even
                turned[slot][top, imag] = ui * even
                turned[slot][low, real] = ui * odd
                turned[slot][low, imag] = ur * minus

    def find(slot):
        sums = jnp.dot(turned[slot][...], both_ref[...], preferred_element_type=jnp.float32)
        found[slot][...] = jnp.transpose(sums.astype(jnp.bfloat16))

    def spread(slot, block):
        wide = 8 * terms
        for piece in range(BLOCK // PIECE):
            start = 2 * piece * PIECE * terms
            stacked = jnp.concatenate(
                [
                    found[slot][:, k : k + wide]
                    for k in range(start, start + 2 * PIECE * terms, wide)
                ],
                axis=0,
            )
            lagged = jnp.dot(
                stacked, spread_ref[...], preferred_element_type=jnp.float32
            ).astype(jnp.bfloat16)
            unit = block * (BLOCK // PIECE) + piece
            for k in range(PIECE):
                for r in range(2):
                    top = (k // 4 * 2 + r) * CH
                    lane = k % 4 * lags
                    out_ref[unit, r, k] = lagged[top : top + CH, lane : lane + lags]
            write(unit).start()

    def write(unit):
        return pltpu.make_async_copy(
            out_ref.at[unit], out_hbm.at[:, pl.ds(unit * PIECE, PIECE)], sems.at[unit]
        )

    half = CH // 2
    loads = [
        pltpu.make_async_copy(source, near_ref.at[pl.ds(k * half, half)], loaded.at[k])
        for k, source in enumerate(partners)
    ]
    for copy in loads:
        copy.start()
    wide_ref[:half, :] = own_low[...].astype(jnp.float32)
    wide_ref[half:, :] = own_high[...].astype(jnp.float32)
    turn(0, 0)
    for copy in loads:
        copy.wait()
    at = pl.multiple_of(order_ref[0] * CH, CH)
    both_ref[:, pl.ds(at, CH)] = jnp.transpose(near_ref[:CH, :])
    both_ref[:, pl.ds(CH - at, CH)] = jnp.transpose(near_ref[CH:, :])
    turn(1, 1)
    find(0)
    for block in range(1, blocks):
        if block + 1 < blocks:
            turn(block + 1, (block + 1) % 2)
        find(block % 2)
        spread((block - 1) % 2, block - 1)
    spread((blocks - 1) % 2, blocks - 1)
    for unit in range(CH // PIECE):
        write(unit).wait()


def correlate(order, own, first, second, nfft, lags):
    depth = own[0].shape[1]
    bins = depth // (2 * W)
    rows, spread = lag_tables(nfft, bins, lags, 1.0 / math.sqrt(W * bins))
    terms = rows.shape[0] // 3
    vmem = pl.BlockSpec(memory_space=pltpu.VMEM)
    return pl.pallas_call(
        correlate_kernel,
        in_specs=[pl.BlockSpec(memory_space=pltpu.SMEM)]
        + [vmem] * 4
        + [pl.BlockSpec(memory_space=pltpu.HBM)] * 4,
        out_specs=pl.BlockSpec(memory_space=pltpu.HBM),
        out_shape=jax.ShapeDtypeStruct((2, CH, CH, lags), jnp.bfloat16),
        scratch_shapes=[
            pltpu.VMEM((depth, 2 * CH), jnp.bfloat16),
            pltpu.VMEM((CH, depth), jnp.float32),
            pltpu.VMEM((2 * CH, depth), jnp.bfloat16),
            pltpu.VMEM((BLOCK * 2 * terms, depth), jnp.bfloat16),
            pltpu.VMEM((BLOCK * 2 * terms, depth), jnp.bfloat16),
            pltpu.VMEM((2 * CH, BLOCK * 2 * terms), jnp.bfloat16),
            pltpu.VMEM((2 * CH, BLOCK * 2 * terms), jnp.bfloat16),
            pltpu.VMEM((CH // PIECE, 2, PIECE, CH, lags), jnp.bfloat16),
            pltpu.SemaphoreType.DMA((CH // PIECE,)),
            pltpu.SemaphoreType.DMA((4,)),
        ],
        compiler_params=pltpu.CompilerParams(vmem_limit_bytes=60 * 1024 * 1024),
        name="correlate",
    )(order, *own, jnp.asarray(rows), jnp.asarray(spread), *first, *second)


def swap(block, mask):
    count = lax.axis_size("blk")
    return lax.ppermute(block, "blk", [(low, low ^ mask) for low in range(count)])


def swap_halves(tile, mask):
    return tuple(swap(half, mask) for half in tile)


def exchange(mask, moving):
    count = lax.axis_size("blk")
    full = count - 1
    first = swap_halves(moving, full)
    if 2 * mask >= count:
        return moving, first, swap_halves(first, mask ^ full)
    return moving, first, swap_halves(moving, mask)


def deliver(me, mask, labels, records, plan):
    owners = lax.axis_size("blk")
    held, nfft = records.shape
    capacity = max(16, 2 * held // owners)
    whole = full_plan(capacity, nfft // 128)
    table = jnp.asarray(forward_table(nfft, F))
    if owners > 16:
        plans = (whole,) * owners
        (outgoing,) = pack(me, labels, records, capacity, plans, False)
        arrived = [lax.all_to_all(outgoing, "blk", split_axis=0, concat_axis=0, tiled=True)]
        *tile, branch = whiten(me, mask, arrived, table, capacity, plans, None)
        return tuple(tile), branch
    half = owners // 2
    plans = (whole,) + (plan(capacity, nfft // 128),) * (owners - 1)
    outgoing = pack(me, labels, records, capacity, plans, True)
    places = [half]
    for distance in range(1, half):
        places += [distance, half + distance]
    arrived = [swap(outgoing[distance], distance) for distance in places] + [outgoing[0]]
    places.append(0)
    ordered = tuple(plans[distance] for distance in places)
    *tile, branch = whiten(me, mask, arrived, table, capacity, ordered, places)
    return tuple(tile), branch


def local(records, dest, slot, valid, masks):
    owners = lax.axis_size("blk")
    held, nfft = records.shape
    full = owners - 1
    me = lax.axis_index("blk").astype(jnp.int32).reshape(1)
    mask = (masks[0] + masks[1] - full).reshape(1)
    labels = [label.reshape(1, held) for label in (dest, slot, valid)]
    if owners <= 16:
        tile, branch = deliver(me, mask, labels, records, short_plan)
        known = [functools.partial(exchange, m) for m in range(1, full)]

        def again(tile):
            tile, branch = deliver(me, mask, labels, records, full_plan)
            return lax.switch(branch[0], known, tile)

        own, first, second = lax.switch(branch[0], known + [again], tile)
    else:
        own, _ = deliver(me, mask, labels, records, full_plan)
        second = own
        for bit in range(owners.bit_length() - 1):
            moved = swap_halves(second, 1 << bit)
            flip = mask >> bit & 1 == 1
            second = tuple(jnp.where(flip, new, old) for new, old in zip(moved, second))
        first = swap_halves(own, full)
    order = (masks[:1] != full).astype(jnp.int32)
    return correlate(order, own, first, second, nfft, LAGS)


def solution(mesh):
    return jax.shard_map(
        local,
        mesh=mesh,
        in_specs=(
            P(("groups", "blk"), None),
            P(("groups", "blk"), None),
            P(("groups", "blk"), None),
            P(("groups", "blk"), None),
            P(),
        ),
        out_specs=P(None, ("groups", "blk"), None, None),
        check_vma=False,
    )
```

profile of v0, /device:TPU:0, one launch (start us, length us, event | category | flops | bytes accessed | tf_op | source)
XLA Modules:
  0.0 77.9 jit_solution(16234333072880928648)
XLA Ops:
  0.0 2.3 %pack.3 = (bf16[520,128]{1,0:T(8,128)(2,1)S(1)}, bf16[448,128]{1,0:T(8,128)(2,1)S(1)}, bf16[448,128]{1,0:T(8,128)(2,1)S(1)}, bf16[448,128]{1,0:T(8,128)(2,1)S(1)...) custom-call(s32[1]{0:T(128)} %bitcast.1.me_ref, ...), custom_call_target="tpu_custom_call" | custom-call | tf_op jit(solution)/shard_map/pack/pallas_call | solution.py:174
  2.3 4.1 %collective-permute-start.127 = (bf16[448,128]{1,0:T(8,128)(2,1)S(1)}, bf16[448,128]{1,0:T(8,128)(2,1)S(1)}, u32[]{:S(2)}, u32[]{:S(2)}) collective-permute-start(bf16[448,128]{1,0:T(8,128)(2,1)S(1)} %get-tuple-element.242), channel_id=1, source_target_pairs={{0,8},{1,9},{2,10},{3,11},{4,12},{5,13},{6,14},{7,15},{8,0},{9,1},... | collective-permute-start | bytes 344072 | tf_op jit(solution)/shard_map/ppermute | solution.py:451
  6.4 0.0 collective-permute-start.128
  6.4 0.2 collective-permute-start.129
  6.6 1.8 %collective-permute-start.130 = (bf16[448,128]{1,0:T(8,128)(2,1)S(1)}, bf16[448,128]{1,0:T(8,128)(2,1)S(1)}, u32[]{:S(2)}, u32[]{:S(2)}) collective-permute-start(bf16[448,128]{1,0:T(8,128)(2,1)S(1)} %get-tuple-element.245), channel_id=1, source_target_pairs={{0,2},{1,3},{2,0},{3,1},{4,6},{5,7},{6,4},{7,5},{8,10},{9,11},{10,... | collective-permute-start | bytes 344072 | tf_op jit(solution)/shard_map/ppermute | solution.py:451
  8.4 2.5 %collective-permute-start.131 = (bf16[448,128]{1,0:T(8,128)(2,1)S(1)}, bf16[448,128]{1,0:T(8,128)(2,1)S(1)}, u32[]{:S(2)}, u32[]{:S(2)}) collective-permute-start(bf16[448,128]{1,0:T(8,128)(2,1)S(1)} %get-tuple-element.246), channel_id=1, source_target_pairs={{0,10},{1,11},{2,8},{3,9},{4,14},{5,15},{6,12},{7,13},{8,2},{9,3},... | collective-permute-start | bytes 344072 | tf_op jit(solution)/shard_map/ppermute | solution.py:451
  10.9 6.8 %collective-permute-done.127.refs_0_ = bf16[448,128]{1,0:T(8,128)(2,1)S(1)} collective-permute-done((bf16[448,128]{1,0:T(8,128)(2,1)S(1)}, bf16[448,128]{1,0:T(8,128)(2,1)S(1)}, u32[]{:S(2)}, u32[]{:S(2)}) %collective-permute-start.127) | collective-permute-done | bytes 114720 | tf_op jit(solution)/shard_map/ppermute | solution.py:451
  17.8 0.0 collective-permute-start.132
  17.8 0.0 collective-permute-done.128.refs_1_
  17.8 0.7 collective-permute-start.133
  18.5 0.1 collective-permute-done.129.refs_2_
  18.6 3.8 %collective-permute-start.134 = (bf16[448,128]{1,0:T(8,128)(2,1)S(1)}, bf16[448,128]{1,0:T(8,128)(2,1)S(1)}, u32[]{:S(2)}, u32[]{:S(2)}) collective-permute-start(bf16[448,128]{1,0:T(8,128)(2,1)S(1)} %get-tuple-element.249), channel_id=1, source_target_pairs={{0,4},{1,5},{2,6},{3,7},{4,0},{5,1},{6,2},{7,3},{8,12},{9,13},{10,... | collective-permute-start | bytes 344072 | tf_op jit(solution)/shard_map/ppermute | solution.py:451
  22.3 0.0 collective-permute-done.130.refs_3_
  22.3 1.0 %collective-permute-start.135 = (bf16[448,128]{1,0:T(8,128)(2,1)S(1)}, bf16[448,128]{1,0:T(8,128)(2,1)S(1)}, u32[]{:S(2)}, u32[]{:S(2)}) collective-permute-start(bf16[448,128]{1,0:T(8,128)(2,1)S(1)} %get-tuple-element.250), channel_id=1, source_target_pairs={{0,12},{1,13},{2,14},{3,15},{4,8},{5,9},{6,10},{7,11},{8,4},{9,5},... | collective-permute-start | bytes 344072 | tf_op jit(solution)/shard_map/ppermute | solution.py:451
  23.3 0.0 collective-permute-done.131.refs_4_
  23.4 1.4 %collective-permute-start.136 = (bf16[448,128]{1,0:T(8,128)(2,1)S(1)}, bf16[448,128]{1,0:T(8,128)(2,1)S(1)}, u32[]{:S(2)}, u32[]{:S(2)}) collective-permute-start(bf16[448,128]{1,0:T(8,128)(2,1)S(1)} %get-tuple-element.251), channel_id=1, source_target_pairs={{0,5},{1,4},{2,7},{3,6},{4,1},{5,0},{6,3},{7,2},{8,13},{9,12},{10,... | collective-permute-start | bytes 344072 | tf_op jit(solution)/shard_map/ppermute | solution.py:451
  24.7 0.3 collective-permute-done.132.refs_5_
  25.0 3.5 %collective-permute-start.137 = (bf16[448,128]{1,0:T(8,128)(2,1)S(1)}, bf16[448,128]{1,0:T(8,128)(2,1)S(1)}, u32[]{:S(2)}, u32[]{:S(2)}) collective-permute-start(bf16[448,128]{1,0:T(8,128)(2,1)S(1)} %get-tuple-element.252), channel_id=1, source_target_pairs={{0,13},{1,12},{2,15},{3,14},{4,9},{5,8},{6,11},{7,10},{8,5},{9,4},... | collective-permute-start | bytes 344072 | tf_op jit(solution)/shard_map/ppermute | solution.py:451
  28.5 0.0 collective-permute-done.133.refs_6_
  28.5 2.5 %collective-permute-start.138 = (bf16[448,128]{1,0:T(8,128)(2,1)S(1)}, bf16[448,128]{1,0:T(8,128)(2,1)S(1)}, u32[]{:S(2)}, u32[]{:S(2)}) collective-permute-start(bf16[448,128]{1,0:T(8,128)(2,1)S(1)} %get-tuple-element.253), channel_id=1, source_target_pairs={{0,6},{1,7},{2,4},{3,5},{4,2},{5,3},{6,0},{7,1},{8,14},{9,15},{10,... | collective-permute-start | bytes 344072 | tf_op jit(solution)/shard_map/ppermute | solution.py:451
  31.0 0.0 collective-permute-done.134.refs_7_
  31.0 7.7 %collective-permute-start.139 = (bf16[448,128]{1,0:T(8,128)(2,1)S(1)}, bf16[448,128]{1,0:T(8,128)(2,1)S(1)}, u32[]{:S(2)}, u32[]{:S(2)}) collective-permute-start(bf16[448,128]{1,0:T(8,128)(2,1)S(1)} %get-tuple-element.254), channel_id=1, source_target_pairs={{0,14},{1,15},{2,12},{3,13},{4,10},{5,11},{6,8},{7,9},{8,6},{9,7},... | collective-permute-start | bytes 344072 | tf_op jit(solution)/shard_map/ppermute | solution.py:451
  38.7 0.0 collective-permute-done.135.refs_8_
  38.7 0.0 collective-permute-start.140
  38.7 0.0 collective-permute-done.136.refs_9_
  38.7 3.4 %collective-permute-start.141 = (bf16[448,128]{1,0:T(8,128)(2,1)S(1)}, bf16[448,128]{1,0:T(8,128)(2,1)S(1)}, u32[]{:S(2)}, u32[]{:S(2)}) collective-permute-start(bf16[448,128]{1,0:T(8,128)(2,1)S(1)} %get-tuple-element.256), channel_id=1, source_target_pairs={{0,15},{1,14},{2,13},{3,12},{4,11},{5,10},{6,9},{7,8},{8,7},{9,6},... | collective-permute-start | bytes 344072 | tf_op jit(solution)/shard_map/ppermute | solution.py:451
  42.1 1.3 %fusion = (s32[1]{0:T(128)}, s32[1]{0:T(128)}) fusion(s32[2]{0:T(128)} %param.42), kind=kLoop, calls=%fused_computation | loop fusion | bytes 16 | tf_op jit(solution)/shard_map/slice | solution.py:497
  45.3 0.0 collective-permute-done.137.refs_10_
  45.3 0.0 collective-permute-done.138.refs_11_
  45.3 0.0 collective-permute-done.139.refs_12_
  45.3 0.2 collective-permute-done.140.refs_13_
  45.5 1.6 %collective-permute-done.141.refs_14_ = bf16[448,128]{1,0:T(8,128)(2,1)S(1)} collective-permute-done((bf16[448,128]{1,0:T(8,128)(2,1)S(1)}, bf16[448,128]{1,0:T(8,128)(2,1)S(1)}, u32[]{:S(2)}, u32[]{:S(2)}) %collective-permute-start.141) | collective-permute-done | bytes 114720 | tf_op jit(solution)/shard_map/ppermute | solution.py:451
  47.1 3.1 %whiten.3 = (bf16[64,1024]{1,0:T(8,128)(2,1)S(1)}, bf16[64,1024]{1,0:T(8,128)(2,1)S(1)}, s32[1]{0:T(128)}) custom-call(s32[1]{0:T(128)} %bitcast.1.me_ref, s32[1]{0:T(128)} %sub.3.mask_ref, bf16[448,128]{1,0:T(8,128)(2,1)S(1)} %collective-permute-done.127.refs_0_, bf16[448,128]{1,0:T(8,128)(2,1)S(1)} %collective-permute-done.128.refs_1_, ...), custom_call_target="tpu_custom_call" | custom-call | tf_op jit(solution)/shard_map/whiten/pallas_call | solution.py:307
  50.8 16.6 %conditional.2 = (bf16[64,1024]{1,0:T(8,128)(2,1)}, bf16[64,1024]{1,0:T(8,128)(2,1)}, bf16[64,1024]{1,0:T(8,128)(2,1)}, bf16[64,1024]{1,0:T(8,128)(2,1)}, bf16[6...) conditional(s32[]{:T(128)} %bitcast.5, (bf16[64,1024]{1,0:T(8,128)(2,1)S(1)}, ...), branch_computations={%region_0.0_spmd, %region_1.0_spmd, %region_2.0_spmd, %region_3.0_... | conditional | flops 1 | bytes 10085224 | solution.py:507
  50.8 0.8 %collective-permute-start.18 = (bf16[64,1024]{1,0:T(8,128)(2,1)S(1)}, bf16[64,1024]{1,0:T(8,128)(2,1)}, u32[]{:S(2)}, u32[]{:S(2)}) collective-permute-start(bf16[64,1024]{1,0:T(8,128)(2,1)S(1)} %get-tuple-element.349), channel_id=1, source_target_pairs={{0,5},{1,4},{2,7},{3,6},{4,1},{5,0},{6,3},{7,2},{8,13},{9,12},{10,... | collective-permute-start | bytes 393224 | tf_op jit(solution)/shard_map/cond/branch_4_fun/ppermute | solution.py:451
  51.7 3.0 %collective-permute-start.16 = (bf16[64,1024]{1,0:T(8,128)(2,1)S(1)}, bf16[64,1024]{1,0:T(8,128)(2,1)}, u32[]{:S(2)}, u32[]{:S(2)}) collective-permute-start(bf16[64,1024]{1,0:T(8,128)(2,1)S(1)} %get-tuple-element.349), channel_id=1, source_target_pairs={{0,15},{1,14},{2,13},{3,12},{4,11},{5,10},{6,9},{7,8},{8,7},{9,6},... | collective-permute-start | bytes 393224 | tf_op jit(solution)/shard_map/cond/branch_4_fun/ppermute | solution.py:451
  54.7 0.8 collective-permute-start.19
  55.5 0.9 %collective-permute-start.17 = (bf16[64,1024]{1,0:T(8,128)(2,1)S(1)}, bf16[64,1024]{1,0:T(8,128)(2,1)}, u32[]{:S(2)}, u32[]{:S(2)}) collective-permute-start(bf16[64,1024]{1,0:T(8,128)(2,1)S(1)} %get-tuple-element.350), channel_id=1, source_target_pairs={{0,15},{1,14},{2,13},{3,12},{4,11},{5,10},{6,9},{7,8},{8,7},{9,6},... | collective-permute-start | bytes 393224 | tf_op jit(solution)/shard_map/cond/branch_4_fun/ppermute | solution.py:451
  56.4 0.7 copy.90
  57.0 0.6 copy.91
  57.7 0.0 collective-permute-done.18
  57.7 4.1 %collective-permute-done.16 = bf16[64,1024]{1,0:T(8,128)(2,1)} collective-permute-done((bf16[64,1024]{1,0:T(8,128)(2,1)S(1)}, bf16[64,1024]{1,0:T(8,128)(2,1)}, u32[]{:S(2)}, u32[]{:S(2)}) %collective-permute-start.16) | collective-permute-done | bytes 131104 | tf_op jit(solution)/shard_map/cond/branch_4_fun/ppermute | solution.py:451
  61.8 1.6 %collective-permute-done.19 = bf16[64,1024]{1,0:T(8,128)(2,1)} collective-permute-done((bf16[64,1024]{1,0:T(8,128)(2,1)S(1)}, bf16[64,1024]{1,0:T(8,128)(2,1)}, u32[]{:S(2)}, u32[]{:S(2)}) %collective-permute-start.19) | collective-permute-done | bytes 131104 | tf_op jit(solution)/shard_map/cond/branch_4_fun/ppermute | solution.py:451
  63.4 4.0 %collective-permute-done.17 = bf16[64,1024]{1,0:T(8,128)(2,1)} collective-permute-done((bf16[64,1024]{1,0:T(8,128)(2,1)S(1)}, bf16[64,1024]{1,0:T(8,128)(2,1)}, u32[]{:S(2)}, u32[]{:S(2)}) %collective-permute-start.17) | collective-permute-done | bytes 131104 | tf_op jit(solution)/shard_map/cond/branch_4_fun/ppermute | solution.py:451
  67.4 10.3 %correlate.1 = bf16[2,128,128,128]{3,2,1,0:T(8,128)(2,1)} custom-call(s32[1]{0:T(128)S(6)} %convert_element_type.3.order_ref, bf16[64,1024]{1,0:T(8,128)(2,1)} %get-tuple-element.261.own_low, bf16[64,1024]{1,0:T(8,128)(2,1)} %get-tuple-element.262.own_high, bf16[96,256]{1,0:T(8,128)(2,1)} %constant.29.clone.rows_ref, ...), custom_call_target="tpu_custom_call" | custom-call | tf_op jit(solution)/shard_map/correlate/pallas_call | solution.py:425
Async XLA Ops:
  2.3 15.4 %collective-permute-start.127 = (bf16[448,128]{1,0:T(8,128)(2,1)S(1)}, bf16[448,128]{1,0:T(8,128)(2,1)S(1)}, u32[]{:S(2)}, u32[]{:S(2)}) collective-permute-start(bf16[448,128]{1,0:T(8,128)(2,1)S(1)} %get-tuple-element.242), channel_id=1, source_target_pairs={{0,8},{1,9},{2,10},{3,11},{4,12},{5,13},{6,14},{7,15},{8,0},{9,1},... | collective-permute-start | bytes 344072 | tf_op jit(solution)/shard_map/ppermute | solution.py:451
  6.4 11.4 %collective-permute-start.128 = (bf16[448,128]{1,0:T(8,128)(2,1)S(1)}, bf16[448,128]{1,0:T(8,128)(2,1)S(1)}, u32[]{:S(2)}, u32[]{:S(2)}) collective-permute-start(bf16[448,128]{1,0:T(8,128)(2,1)S(1)} %get-tuple-element.243), channel_id=1, source_target_pairs={{0,1},{1,0},{2,3},{3,2},{4,5},{5,4},{6,7},{7,6},{8,9},{9,8},{10,11... | collective-permute-start | bytes 344072 | tf_op jit(solution)/shard_map/ppermute | solution.py:451
  6.4 12.2 %collective-permute-start.129 = (bf16[448,128]{1,0:T(8,128)(2,1)S(1)}, bf16[448,128]{1,0:T(8,128)(2,1)S(1)}, u32[]{:S(2)}, u32[]{:S(2)}) collective-permute-start(bf16[448,128]{1,0:T(8,128)(2,1)S(1)} %get-tuple-element.244), channel_id=1, source_target_pairs={{0,9},{1,8},{2,11},{3,10},{4,13},{5,12},{6,15},{7,14},{8,1},{9,0},... | collective-permute-start | bytes 344072 | tf_op jit(solution)/shard_map/ppermute | solution.py:451
  6.6 15.7 %collective-permute-start.130 = (bf16[448,128]{1,0:T(8,128)(2,1)S(1)}, bf16[448,128]{1,0:T(8,128)(2,1)S(1)}, u32[]{:S(2)}, u32[]{:S(2)}) collective-permute-start(bf16[448,128]{1,0:T(8,128)(2,1)S(1)} %get-tuple-element.245), channel_id=1, source_target_pairs={{0,2},{1,3},{2,0},{3,1},{4,6},{5,7},{6,4},{7,5},{8,10},{9,11},{10,... | collective-permute-start | bytes 344072 | tf_op jit(solution)/shard_map/ppermute | solution.py:451
  8.4 14.9 %collective-permute-start.131 = (bf16[448,128]{1,0:T(8,128)(2,1)S(1)}, bf16[448,128]{1,0:T(8,128)(2,1)S(1)}, u32[]{:S(2)}, u32[]{:S(2)}) collective-permute-start(bf16[448,128]{1,0:T(8,128)(2,1)S(1)} %get-tuple-element.246), channel_id=1, source_target_pairs={{0,10},{1,11},{2,8},{3,9},{4,14},{5,15},{6,12},{7,13},{8,2},{9,3},... | collective-permute-start | bytes 344072 | tf_op jit(solution)/shard_map/ppermute | solution.py:451
  17.8 7.2 %collective-permute-start.132 = (bf16[448,128]{1,0:T(8,128)(2,1)S(1)}, bf16[448,128]{1,0:T(8,128)(2,1)S(1)}, u32[]{:S(2)}, u32[]{:S(2)}) collective-permute-start(bf16[448,128]{1,0:T(8,128)(2,1)S(1)} %get-tuple-element.247), channel_id=1, source_target_pairs={{0,3},{1,2},{2,1},{3,0},{4,7},{5,6},{6,5},{7,4},{8,11},{9,10},{10,... | collective-permute-start | bytes 344072 | tf_op jit(solution)/shard_map/ppermute | solution.py:451
  17.8 10.7 %collective-permute-start.133 = (bf16[448,128]{1,0:T(8,128)(2,1)S(1)}, bf16[448,128]{1,0:T(8,128)(2,1)S(1)}, u32[]{:S(2)}, u32[]{:S(2)}) collective-permute-start(bf16[448,128]{1,0:T(8,128)(2,1)S(1)} %get-tuple-element.248), channel_id=1, source_target_pairs={{0,11},{1,10},{2,9},{3,8},{4,15},{5,14},{6,13},{7,12},{8,3},{9,2},... | collective-permute-start | bytes 344072 | tf_op jit(solution)/shard_map/ppermute | solution.py:451
  18.6 12.4 %collective-permute-start.134 = (bf16[448,128]{1,0:T(8,128)(2,1)S(1)}, bf16[448,128]{1,0:T(8,128)(2,1)S(1)}, u32[]{:S(2)}, u32[]{:S(2)}) collective-permute-start(bf16[448,128]{1,0:T(8,128)(2,1)S(1)} %get-tuple-element.249), channel_id=1, source_target_pairs={{0,4},{1,5},{2,6},{3,7},{4,0},{5,1},{6,2},{7,3},{8,12},{9,13},{10,... | collective-permute-start | bytes 344072 | tf_op jit(solution)/shard_map/ppermute | solution.py:451
  22.3 16.4 %collective-permute-start.135 = (bf16[448,128]{1,0:T(8,128)(2,1)S(1)}, bf16[448,128]{1,0:T(8,128)(2,1)S(1)}, u32[]{:S(2)}, u32[]{:S(2)}) collective-permute-start(bf16[448,128]{1,0:T(8,128)(2,1)S(1)} %get-tuple-element.250), channel_id=1, source_target_pairs={{0,12},{1,13},{2,14},{3,15},{4,8},{5,9},{6,10},{7,11},{8,4},{9,5},... | collective-permute-start | bytes 344072 | tf_op jit(solution)/shard_map/ppermute | solution.py:451
  23.4 15.3 %collective-permute-start.136 = (bf16[448,128]{1,0:T(8,128)(2,1)S(1)}, bf16[448,128]{1,0:T(8,128)(2,1)S(1)}, u32[]{:S(2)}, u32[]{:S(2)}) collective-permute-start(bf16[448,128]{1,0:T(8,128)(2,1)S(1)} %get-tuple-element.251), channel_id=1, source_target_pairs={{0,5},{1,4},{2,7},{3,6},{4,1},{5,0},{6,3},{7,2},{8,13},{9,12},{10,... | collective-permute-start | bytes 344072 | tf_op jit(solution)/shard_map/ppermute | solution.py:451
  25.0 20.3 %collective-permute-start.137 = (bf16[448,128]{1,0:T(8,128)(2,1)S(1)}, bf16[448,128]{1,0:T(8,128)(2,1)S(1)}, u32[]{:S(2)}, u32[]{:S(2)}) collective-permute-start(bf16[448,128]{1,0:T(8,128)(2,1)S(1)} %get-tuple-element.252), channel_id=1, source_target_pairs={{0,13},{1,12},{2,15},{3,14},{4,9},{5,8},{6,11},{7,10},{8,5},{9,4},... | collective-permute-start | bytes 344072 | tf_op jit(solution)/shard_map/ppermute | solution.py:451
  28.5 16.9 %collective-permute-start.138 = (bf16[448,128]{1,0:T(8,128)(2,1)S(1)}, bf16[448,128]{1,0:T(8,128)(2,1)S(1)}, u32[]{:S(2)}, u32[]{:S(2)}) collective-permute-start(bf16[448,128]{1,0:T(8,128)(2,1)S(1)} %get-tuple-element.253), channel_id=1, source_target_pairs={{0,6},{1,7},{2,4},{3,5},{4,2},{5,3},{6,0},{7,1},{8,14},{9,15},{10,... | collective-permute-start | bytes 344072 | tf_op jit(solution)/shard_map/ppermute | solution.py:451
  31.0 14.4 %collective-permute-start.139 = (bf16[448,128]{1,0:T(8,128)(2,1)S(1)}, bf16[448,128]{1,0:T(8,128)(2,1)S(1)}, u32[]{:S(2)}, u32[]{:S(2)}) collective-permute-start(bf16[448,128]{1,0:T(8,128)(2,1)S(1)} %get-tuple-element.254), channel_id=1, source_target_pairs={{0,14},{1,15},{2,12},{3,13},{4,10},{5,11},{6,8},{7,9},{8,6},{9,7},... | collective-permute-start | bytes 344072 | tf_op jit(solution)/shard_map/ppermute | solution.py:451
  38.7 6.8 %collective-permute-start.140 = (bf16[448,128]{1,0:T(8,128)(2,1)S(1)}, bf16[448,128]{1,0:T(8,128)(2,1)S(1)}, u32[]{:S(2)}, u32[]{:S(2)}) collective-permute-start(bf16[448,128]{1,0:T(8,128)(2,1)S(1)} %get-tuple-element.255), channel_id=1, source_target_pairs={{0,7},{1,6},{2,5},{3,4},{4,3},{5,2},{6,1},{7,0},{8,15},{9,14},{10,... | collective-permute-start | bytes 344072 | tf_op jit(solution)/shard_map/ppermute | solution.py:451
  38.7 8.4 %collective-permute-start.141 = (bf16[448,128]{1,0:T(8,128)(2,1)S(1)}, bf16[448,128]{1,0:T(8,128)(2,1)S(1)}, u32[]{:S(2)}, u32[]{:S(2)}) collective-permute-start(bf16[448,128]{1,0:T(8,128)(2,1)S(1)} %get-tuple-element.256), channel_id=1, source_target_pairs={{0,15},{1,14},{2,13},{3,12},{4,11},{5,10},{6,9},{7,8},{8,7},{9,6},... | collective-permute-start | bytes 344072 | tf_op jit(solution)/shard_map/ppermute | solution.py:451
  50.8 6.8 %collective-permute-start.18 = (bf16[64,1024]{1,0:T(8,128)(2,1)S(1)}, bf16[64,1024]{1,0:T(8,128)(2,1)}, u32[]{:S(2)}, u32[]{:S(2)}) collective-permute-start(bf16[64,1024]{1,0:T(8,128)(2,1)S(1)} %get-tuple-element.349), channel_id=1, source_target_pairs={{0,5},{1,4},{2,7},{3,6},{4,1},{5,0},{6,3},{7,2},{8,13},{9,12},{10,... | collective-permute-start | bytes 393224 | tf_op jit(solution)/shard_map/cond/branch_4_fun/ppermute | solution.py:451
  51.7 10.1 %collective-permute-start.16 = (bf16[64,1024]{1,0:T(8,128)(2,1)S(1)}, bf16[64,1024]{1,0:T(8,128)(2,1)}, u32[]{:S(2)}, u32[]{:S(2)}) collective-permute-start(bf16[64,1024]{1,0:T(8,128)(2,1)S(1)} %get-tuple-element.349), channel_id=1, source_target_pairs={{0,15},{1,14},{2,13},{3,12},{4,11},{5,10},{6,9},{7,8},{8,7},{9,6},... | collective-permute-start | bytes 393224 | tf_op jit(solution)/shard_map/cond/branch_4_fun/ppermute | solution.py:451
  54.7 8.7 %collective-permute-start.19 = (bf16[64,1024]{1,0:T(8,128)(2,1)S(1)}, bf16[64,1024]{1,0:T(8,128)(2,1)}, u32[]{:S(2)}, u32[]{:S(2)}) collective-permute-start(bf16[64,1024]{1,0:T(8,128)(2,1)S(1)} %get-tuple-element.350), channel_id=1, source_target_pairs={{0,5},{1,4},{2,7},{3,6},{4,1},{5,0},{6,3},{7,2},{8,13},{9,12},{10,... | collective-permute-start | bytes 393224 | tf_op jit(solution)/shard_map/cond/branch_4_fun/ppermute | solution.py:451
  55.5 11.9 %collective-permute-start.17 = (bf16[64,1024]{1,0:T(8,128)(2,1)S(1)}, bf16[64,1024]{1,0:T(8,128)(2,1)}, u32[]{:S(2)}, u32[]{:S(2)}) collective-permute-start(bf16[64,1024]{1,0:T(8,128)(2,1)S(1)} %get-tuple-element.350), channel_id=1, source_target_pairs={{0,15},{1,14},{2,13},{3,12},{4,11},{5,10},{6,9},{7,8},{8,7},{9,6},... | collective-permute-start | bytes 393224 | tf_op jit(solution)/shard_map/cond/branch_4_fun/ppermute | solution.py:451
where the time goes:
time: 78.1 us; the launch traced here: 77.9 us
  starting transfers between devices  38 us (49%)
  waiting for transfers between devices  18.7 us (24%)
  Pallas kernels  15.7 us (20%)
  between operations  2.77 us (4%)
  local copies, waits for them, and re-layouts  2.6 us (3%)
    ppermute x19, starting transfers between devices, swap(): lax.ppermute(block, 'blk', [(low, low ^ mask) for low in range(count)])  38 us
    ppermute x19, waiting for transfers between devices, swap(): lax.ppermute(block, 'blk', [(low, low ^ mask) for low in range(count)])  18.7 us
    pallas_call x1, Pallas kernels, correlate(): pl.pallas_call(correlate_kernel, in_specs=[pl.BlockSpec(memory_space=pltp...  10.3 us
    pallas_call x1, Pallas kernels, whiten(): pl.pallas_call(functools.partial(whiten_kernel, capacity, plans, places),...  3.05 us
    pallas_call x1, Pallas kernels, pack(): pl.pallas_call(functools.partial(pack_kernel, owners, capacity, plans), i...  2.33 us
  transfers between devices with their start and end apart: 19, of which 8 were waited for; matrix products, arithmetic and copies ran while one was open for 3% of the time, Pallas kernels for 0%

commit v1 on v0

--- a/solution.py
+++ b/solution.py
@@ -326,7 +326,7 @@
     )(me, mask, *arrived, table)
 
 
-BLOCK = 32
+BLOCK = 64
 PIECE = 16
 
 
@@ -460,8 +460,8 @@
     full = count - 1
     first = swap_halves(moving, full)
     if 2 * mask >= count:
-        return moving, first, swap_halves(first, mask ^ full)
-    return moving, first, swap_halves(moving, mask)
+        return moving, swap_halves(first, mask ^ full), first
+    return moving, swap_halves(moving, mask), first
 
 
 def deliver(me, mask, labels, records, plan):
@@ -504,7 +504,7 @@
             tile, branch = deliver(me, mask, labels, records, full_plan)
             return lax.switch(branch[0], known, tile)
 
-        own, first, second = lax.switch(branch[0], known + [again], tile)
+        own, second, first = lax.switch(branch[0], known + [again], tile)
     else:
         own, _ = deliver(me, mask, labels, records, full_plan)
         second = own

time: 78.1 us -> 80.5 us (1.031)
  waiting for transfers between devices: 18.7 us -> 20.6 us
    ppermute x19, waiting for transfers between devices: 18.7 us -> 20.6 us  [swap(): lax.ppermute(block, 'blk', [(low, low ^ mask) for low in range(count)])]
  transfers between devices with their start and end apart: 19 -> 19, of which waited for: 8 -> 9; matrix products, arithmetic and copies ran while one was open for 3% -> 3% of each run, Pallas kernels for 0% -> 0%
where the time goes in v1:
time: 80.5 us; the launch traced here: 80.2 us
  starting transfers between devices  38.1 us (47%)
  waiting for transfers between devices  20.6 us (26%)
  Pallas kernels  16 us (20%)
  between operations  2.77 us (3%)
  local copies, waits for them, and re-layouts  2.6 us (3%)
    ppermute x19, starting transfers between devices, swap(): lax.ppermute(block, 'blk', [(low, low ^ mask) for low in range(count)])  38.1 us
    ppermute x19, waiting for transfers between devices, swap(): lax.ppermute(block, 'blk', [(low, low ^ mask) for low in range(count)])  20.6 us
    pallas_call x1, Pallas kernels, correlate(): pl.pallas_call(correlate_kernel, in_specs=[pl.BlockSpec(memory_space=pltp...  10.6 us
    pallas_call x1, Pallas kernels, whiten(): pl.pallas_call(functools.partial(whiten_kernel, capacity, plans, places),...  3.05 us
    pallas_call x1, Pallas kernels, pack(): pl.pallas_call(functools.partial(pack_kernel, owners, capacity, plans), i...  2.33 us
  transfers between devices with their start and end apart: 19, of which 9 were waited for; matrix products, arithmetic and copies ran while one was open for 3% of the time, Pallas kernels for 0%

profile of v1, /device:TPU:0, one launch (start us, length us, event | category | flops | bytes accessed | tf_op | source)
XLA Modules:
  0.0 80.2 jit_solution(2264653287527293522)
XLA Ops:
  0.0 2.3 %pack.3 = (bf16[520,128]{1,0:T(8,128)(2,1)S(1)}, bf16[448,128]{1,0:T(8,128)(2,1)S(1)}, bf16[448,128]{1,0:T(8,128)(2,1)S(1)}, bf16[448,128]{1,0:T(8,128)(2,1)S(1)...) custom-call(s32[1]{0:T(128)} %bitcast.1.me_ref, ...), custom_call_target="tpu_custom_call" | custom-call | tf_op jit(solution)/shard_map/pack/pallas_call | solution.py:174
  2.3 4.1 %collective-permute-start.127 = (bf16[448,128]{1,0:T(8,128)(2,1)S(1)}, bf16[448,128]{1,0:T(8,128)(2,1)S(1)}, u32[]{:S(2)}, u32[]{:S(2)}) collective-permute-start(bf16[448,128]{1,0:T(8,128)(2,1)S(1)} %get-tuple-element.242), channel_id=1, source_target_pairs={{0,8},{1,9},{2,10},{3,11},{4,12},{5,13},{6,14},{7,15},{8,0},{9,1},... | collective-permute-start | bytes 344072 | tf_op jit(solution)/shard_map/ppermute | solution.py:451
  6.4 0.0 collective-permute-start.128
  6.4 0.2 collective-permute-start.129
  6.6 1.8 %collective-permute-start.130 = (bf16[448,128]{1,0:T(8,128)(2,1)S(1)}, bf16[448,128]{1,0:T(8,128)(2,1)S(1)}, u32[]{:S(2)}, u32[]{:S(2)}) collective-permute-start(bf16[448,128]{1,0:T(8,128)(2,1)S(1)} %get-tuple-element.245), channel_id=1, source_target_pairs={{0,2},{1,3},{2,0},{3,1},{4,6},{5,7},{6,4},{7,5},{8,10},{9,11},{10,... | collective-permute-start | bytes 344072 | tf_op jit(solution)/shard_map/ppermute | solution.py:451
  8.4 2.5 %collective-permute-start.131 = (bf16[448,128]{1,0:T(8,128)(2,1)S(1)}, bf16[448,128]{1,0:T(8,128)(2,1)S(1)}, u32[]{:S(2)}, u32[]{:S(2)}) collective-permute-start(bf16[448,128]{1,0:T(8,128)(2,1)S(1)} %get-tuple-element.246), channel_id=1, source_target_pairs={{0,10},{1,11},{2,8},{3,9},{4,14},{5,15},{6,12},{7,13},{8,2},{9,3},... | collective-permute-start | bytes 344072 | tf_op jit(solution)/shard_map/ppermute | solution.py:451
  10.9 6.8 %collective-permute-done.127.refs_0_ = bf16[448,128]{1,0:T(8,128)(2,1)S(1)} collective-permute-done((bf16[448,128]{1,0:T(8,128)(2,1)S(1)}, bf16[448,128]{1,0:T(8,128)(2,1)S(1)}, u32[]{:S(2)}, u32[]{:S(2)}) %collective-permute-start.127) | collective-permute-done | bytes 114720 | tf_op jit(solution)/shard_map/ppermute | solution.py:451
  17.8 0.0 collective-permute-start.132
  17.8 0.0 collective-permute-done.128.refs_1_
  17.8 0.7 collective-permute-start.133
  18.5 0.1 collective-permute-done.129.refs_2_
  18.6 3.8 %collective-permute-start.134 = (bf16[448,128]{1,0:T(8,128)(2,1)S(1)}, bf16[448,128]{1,0:T(8,128)(2,1)S(1)}, u32[]{:S(2)}, u32[]{:S(2)}) collective-permute-start(bf16[448,128]{1,0:T(8,128)(2,1)S(1)} %get-tuple-element.249), channel_id=1, source_target_pairs={{0,4},{1,5},{2,6},{3,7},{4,0},{5,1},{6,2},{7,3},{8,12},{9,13},{10,... | collective-permute-start | bytes 344072 | tf_op jit(solution)/shard_map/ppermute | solution.py:451
  22.3 0.0 collective-permute-done.130.refs_3_
  22.3 1.0 %collective-permute-start.135 = (bf16[448,128]{1,0:T(8,128)(2,1)S(1)}, bf16[448,128]{1,0:T(8,128)(2,1)S(1)}, u32[]{:S(2)}, u32[]{:S(2)}) collective-permute-start(bf16[448,128]{1,0:T(8,128)(2,1)S(1)} %get-tuple-element.250), channel_id=1, source_target_pairs={{0,12},{1,13},{2,14},{3,15},{4,8},{5,9},{6,10},{7,11},{8,4},{9,5},... | collective-permute-start | bytes 344072 | tf_op jit(solution)/shard_map/ppermute | solution.py:451
  23.3 0.0 collective-permute-done.131.refs_4_
  23.4 1.4 %collective-permute-start.136 = (bf16[448,128]{1,0:T(8,128)(2,1)S(1)}, bf16[448,128]{1,0:T(8,128)(2,1)S(1)}, u32[]{:S(2)}, u32[]{:S(2)}) collective-permute-start(bf16[448,128]{1,0:T(8,128)(2,1)S(1)} %get-tuple-element.251), channel_id=1, source_target_pairs={{0,5},{1,4},{2,7},{3,6},{4,1},{5,0},{6,3},{7,2},{8,13},{9,12},{10,... | collective-permute-start | bytes 344072 | tf_op jit(solution)/shard_map/ppermute | solution.py:451
  24.7 0.3 collective-permute-done.132.refs_5_
  25.0 3.5 %collective-permute-start.137 = (bf16[448,128]{1,0:T(8,128)(2,1)S(1)}, bf16[448,128]{1,0:T(8,128)(2,1)S(1)}, u32[]{:S(2)}, u32[]{:S(2)}) collective-permute-start(bf16[448,128]{1,0:T(8,128)(2,1)S(1)} %get-tuple-element.252), channel_id=1, source_target_pairs={{0,13},{1,12},{2,15},{3,14},{4,9},{5,8},{6,11},{7,10},{8,5},{9,4},... | collective-permute-start | bytes 344072 | tf_op jit(solution)/shard_map/ppermute | solution.py:451
  28.5 0.0 collective-permute-done.133.refs_6_
  28.5 2.5 %collective-permute-start.138 = (bf16[448,128]{1,0:T(8,128)(2,1)S(1)}, bf16[448,128]{1,0:T(8,128)(2,1)S(1)}, u32[]{:S(2)}, u32[]{:S(2)}) collective-permute-start(bf16[448,128]{1,0:T(8,128)(2,1)S(1)} %get-tuple-element.253), channel_id=1, source_target_pairs={{0,6},{1,7},{2,4},{3,5},{4,2},{5,3},{6,0},{7,1},{8,14},{9,15},{10,... | collective-permute-start | bytes 344072 | tf_op jit(solution)/shard_map/ppermute | solution.py:451
  31.0 0.0 collective-permute-done.134.refs_7_
  31.0 7.7 %collective-permute-start.139 = (bf16[448,128]{1,0:T(8,128)(2,1)S(1)}, bf16[448,128]{1,0:T(8,128)(2,1)S(1)}, u32[]{:S(2)}, u32[]{:S(2)}) collective-permute-start(bf16[448,128]{1,0:T(8,128)(2,1)S(1)} %get-tuple-element.254), channel_id=1, source_target_pairs={{0,14},{1,15},{2,12},{3,13},{4,10},{5,11},{6,8},{7,9},{8,6},{9,7},... | collective-permute-start | bytes 344072 | tf_op jit(solution)/shard_map/ppermute | solution.py:451
  38.7 0.0 collective-permute-done.135.refs_8_
  38.7 0.0 collective-permute-start.140
  38.7 0.0 collective-permute-done.136.refs_9_
  38.7 3.4 %collective-permute-start.141 = (bf16[448,128]{1,0:T(8,128)(2,1)S(1)}, bf16[448,128]{1,0:T(8,128)(2,1)S(1)}, u32[]{:S(2)}, u32[]{:S(2)}) collective-permute-start(bf16[448,128]{1,0:T(8,128)(2,1)S(1)} %get-tuple-element.256), channel_id=1, source_target_pairs={{0,15},{1,14},{2,13},{3,12},{4,11},{5,10},{6,9},{7,8},{8,7},{9,6},... | collective-permute-start | bytes 344072 | tf_op jit(solution)/shard_map/ppermute | solution.py:451
  42.1 1.3 %fusion = (s32[1]{0:T(128)}, s32[1]{0:T(128)}) fusion(s32[2]{0:T(128)} %param.42), kind=kLoop, calls=%fused_computation | loop fusion | bytes 16 | tf_op jit(solution)/shard_map/slice | solution.py:497
  45.3 0.0 collective-permute-done.137.refs_10_
  45.3 0.0 collective-permute-done.138.refs_11_
  45.3 0.0 collective-permute-done.139.refs_12_
  45.3 0.2 collective-permute-done.140.refs_13_
  45.5 1.6 %collective-permute-done.141.refs_14_ = bf16[448,128]{1,0:T(8,128)(2,1)S(1)} collective-permute-done((bf16[448,128]{1,0:T(8,128)(2,1)S(1)}, bf16[448,128]{1,0:T(8,128)(2,1)S(1)}, u32[]{:S(2)}, u32[]{:S(2)}) %collective-permute-start.141) | collective-permute-done | bytes 114720 | tf_op jit(solution)/shard_map/ppermute | solution.py:451
  47.1 3.1 %whiten.3 = (bf16[64,1024]{1,0:T(8,128)(2,1)S(1)}, bf16[64,1024]{1,0:T(8,128)(2,1)S(1)}, s32[1]{0:T(128)}) custom-call(s32[1]{0:T(128)} %bitcast.1.me_ref, s32[1]{0:T(128)} %sub.3.mask_ref, bf16[448,128]{1,0:T(8,128)(2,1)S(1)} %collective-permute-done.127.refs_0_, bf16[448,128]{1,0:T(8,128)(2,1)S(1)} %collective-permute-done.128.refs_1_, ...), custom_call_target="tpu_custom_call" | custom-call | tf_op jit(solution)/shard_map/whiten/pallas_call | solution.py:307
  50.8 18.6 %conditional.2 = (bf16[64,1024]{1,0:T(8,128)(2,1)}, bf16[64,1024]{1,0:T(8,128)(2,1)}, bf16[64,1024]{1,0:T(8,128)(2,1)}, bf16[64,1024]{1,0:T(8,128)(2,1)}, bf16[6...) conditional(s32[]{:T(128)} %bitcast.5, (bf16[64,1024]{1,0:T(8,128)(2,1)S(1)}, ...), branch_computations={%region_0.0_spmd, %region_1.0_spmd, %region_2.0_spmd, %region_3.0_... | conditional | flops 1 | bytes 10085224 | solution.py:507
  50.8 3.8 %collective-permute-start.44 = (bf16[64,1024]{1,0:T(8,128)(2,1)S(1)}, bf16[64,1024]{1,0:T(8,128)(2,1)}, u32[]{:S(2)}, u32[]{:S(2)}) collective-permute-start(bf16[64,1024]{1,0:T(8,128)(2,1)S(1)} %get-tuple-element.391), channel_id=1, source_target_pairs={{0,15},{1,14},{2,13},{3,12},{4,11},{5,10},{6,9},{7,8},{8,7},{9,6},... | collective-permute-start | bytes 393224 | tf_op jit(solution)/shard_map/cond/branch_11_fun/ppermute | solution.py:451
  54.6 0.8 collective-permute-start.46
  55.4 3.8 %collective-permute-done.44 = bf16[64,1024]{1,0:T(8,128)(2,1)} collective-permute-done((bf16[64,1024]{1,0:T(8,128)(2,1)S(1)}, bf16[64,1024]{1,0:T(8,128)(2,1)}, u32[]{:S(2)}, u32[]{:S(2)}) %collective-permute-start.44) | collective-permute-done | bytes 131104 | tf_op jit(solution)/shard_map/cond/branch_11_fun/ppermute | solution.py:451
  59.2 0.4 collective-permute-start.45
  59.5 3.9 %collective-permute-done.46 = bf16[64,1024]{1,0:T(8,128)(2,1)} collective-permute-done((bf16[64,1024]{1,0:T(8,128)(2,1)S(1)}, bf16[64,1024]{1,0:T(8,128)(2,1)}, u32[]{:S(2)}, u32[]{:S(2)}) %collective-permute-start.46) | collective-permute-done | bytes 131104 | tf_op jit(solution)/shard_map/cond/branch_11_fun/ppermute | solution.py:451
  63.4 0.7 collective-permute-start.47
  64.1 0.7 copy.132
  64.8 0.6 copy.133
  65.4 0.7 collective-permute-done.45
  66.1 3.3 %collective-permute-done.47 = bf16[64,1024]{1,0:T(8,128)(2,1)} collective-permute-done((bf16[64,1024]{1,0:T(8,128)(2,1)}, bf16[64,1024]{1,0:T(8,128)(2,1)}, u32[]{:S(2)}, u32[]{:S(2)}) %collective-permute-start.47) | collective-permute-done | bytes 131104 | tf_op jit(solution)/shard_map/cond/branch_11_fun/ppermute | solution.py:451
  69.4 10.6 %correlate.1 = bf16[2,128,128,128]{3,2,1,0:T(8,128)(2,1)} custom-call(s32[1]{0:T(128)S(6)} %convert_element_type.3.order_ref, bf16[64,1024]{1,0:T(8,128)(2,1)} %get-tuple-element.261.own_low, bf16[64,1024]{1,0:T(8,128)(2,1)} %get-tuple-element.262.own_high, bf16[96,256]{1,0:T(8,128)(2,1)} %constant.29.clone.rows_ref, ...), custom_call_target="tpu_custom_call" | custom-call | tf_op jit(solution)/shard_map/correlate/pallas_call | solution.py:425
Async XLA Ops:
  2.3 15.4 %collective-permute-start.127 = (bf16[448,128]{1,0:T(8,128)(2,1)S(1)}, bf16[448,128]{1,0:T(8,128)(2,1)S(1)}, u32[]{:S(2)}, u32[]{:S(2)}) collective-permute-start(bf16[448,128]{1,0:T(8,128)(2,1)S(1)} %get-tuple-element.242), channel_id=1, source_target_pairs={{0,8},{1,9},{2,10},{3,11},{4,12},{5,13},{6,14},{7,15},{8,0},{9,1},... | collective-permute-start | bytes 344072 | tf_op jit(solution)/shard_map/ppermute | solution.py:451
  6.4 11.4 %collective-permute-start.128 = (bf16[448,128]{1,0:T(8,128)(2,1)S(1)}, bf16[448,128]{1,0:T(8,128)(2,1)S(1)}, u32[]{:S(2)}, u32[]{:S(2)}) collective-permute-start(bf16[448,128]{1,0:T(8,128)(2,1)S(1)} %get-tuple-element.243), channel_id=1, source_target_pairs={{0,1},{1,0},{2,3},{3,2},{4,5},{5,4},{6,7},{7,6},{8,9},{9,8},{10,11... | collective-permute-start | bytes 344072 | tf_op jit(solution)/shard_map/ppermute | solution.py:451
  6.4 12.2 %collective-permute-start.129 = (bf16[448,128]{1,0:T(8,128)(2,1)S(1)}, bf16[448,128]{1,0:T(8,128)(2,1)S(1)}, u32[]{:S(2)}, u32[]{:S(2)}) collective-permute-start(bf16[448,128]{1,0:T(8,128)(2,1)S(1)} %get-tuple-element.244), channel_id=1, source_target_pairs={{0,9},{1,8},{2,11},{3,10},{4,13},{5,12},{6,15},{7,14},{8,1},{9,0},... | collective-permute-start | bytes 344072 | tf_op jit(solution)/shard_map/ppermute | solution.py:451
  6.6 15.7 %collective-permute-start.130 = (bf16[448,128]{1,0:T(8,128)(2,1)S(1)}, bf16[448,128]{1,0:T(8,128)(2,1)S(1)}, u32[]{:S(2)}, u32[]{:S(2)}) collective-permute-start(bf16[448,128]{1,0:T(8,128)(2,1)S(1)} %get-tuple-element.245), channel_id=1, source_target_pairs={{0,2},{1,3},{2,0},{3,1},{4,6},{5,7},{6,4},{7,5},{8,10},{9,11},{10,... | collective-permute-start | bytes 344072 | tf_op jit(solution)/shard_map/ppermute | solution.py:451
  8.4 14.9 %collective-permute-start.131 = (bf16[448,128]{1,0:T(8,128)(2,1)S(1)}, bf16[448,128]{1,0:T(8,128)(2,1)S(1)}, u32[]{:S(2)}, u32[]{:S(2)}) collective-permute-start(bf16[448,128]{1,0:T(8,128)(2,1)S(1)} %get-tuple-element.246), channel_id=1, source_target_pairs={{0,10},{1,11},{2,8},{3,9},{4,14},{5,15},{6,12},{7,13},{8,2},{9,3},... | collective-permute-start | bytes 344072 | tf_op jit(solution)/shard_map/ppermute | solution.py:451
  17.8 7.2 %collective-permute-start.132 = (bf16[448,128]{1,0:T(8,128)(2,1)S(1)}, bf16[448,128]{1,0:T(8,128)(2,1)S(1)}, u32[]{:S(2)}, u32[]{:S(2)}) collective-permute-start(bf16[448,128]{1,0:T(8,128)(2,1)S(1)} %get-tuple-element.247), channel_id=1, source_target_pairs={{0,3},{1,2},{2,1},{3,0},{4,7},{5,6},{6,5},{7,4},{8,11},{9,10},{10,... | collective-permute-start | bytes 344072 | tf_op jit(solution)/shard_map/ppermute | solution.py:451
  17.8 10.7 %collective-permute-start.133 = (bf16[448,128]{1,0:T(8,128)(2,1)S(1)}, bf16[448,128]{1,0:T(8,128)(2,1)S(1)}, u32[]{:S(2)}, u32[]{:S(2)}) collective-permute-start(bf16[448,128]{1,0:T(8,128)(2,1)S(1)} %get-tuple-element.248), channel_id=1, source_target_pairs={{0,11},{1,10},{2,9},{3,8},{4,15},{5,14},{6,13},{7,12},{8,3},{9,2},... | collective-permute-start | bytes 344072 | tf_op jit(solution)/shard_map/ppermute | solution.py:451
  18.6 12.4 %collective-permute-start.134 = (bf16[448,128]{1,0:T(8,128)(2,1)S(1)}, bf16[448,128]{1,0:T(8,128)(2,1)S(1)}, u32[]{:S(2)}, u32[]{:S(2)}) collective-permute-start(bf16[448,128]{1,0:T(8,128)(2,1)S(1)} %get-tuple-element.249), channel_id=1, source_target_pairs={{0,4},{1,5},{2,6},{3,7},{4,0},{5,1},{6,2},{7,3},{8,12},{9,13},{10,... | collective-permute-start | bytes 344072 | tf_op jit(solution)/shard_map/ppermute | solution.py:451
  22.3 16.4 %collective-permute-start.135 = (bf16[448,128]{1,0:T(8,128)(2,1)S(1)}, bf16[448,128]{1,0:T(8,128)(2,1)S(1)}, u32[]{:S(2)}, u32[]{:S(2)}) collective-permute-start(bf16[448,128]{1,0:T(8,128)(2,1)S(1)} %get-tuple-element.250), channel_id=1, source_target_pairs={{0,12},{1,13},{2,14},{3,15},{4,8},{5,9},{6,10},{7,11},{8,4},{9,5},... | collective-permute-start | bytes 344072 | tf_op jit(solution)/shard_map/ppermute | solution.py:451
  23.4 15.3 %collective-permute-start.136 = (bf16[448,128]{1,0:T(8,128)(2,1)S(1)}, bf16[448,128]{1,0:T(8,128)(2,1)S(1)}, u32[]{:S(2)}, u32[]{:S(2)}) collective-permute-start(bf16[448,128]{1,0:T(8,128)(2,1)S(1)} %get-tuple-element.251), channel_id=1, source_target_pairs={{0,5},{1,4},{2,7},{3,6},{4,1},{5,0},{6,3},{7,2},{8,13},{9,12},{10,... | collective-permute-start | bytes 344072 | tf_op jit(solution)/shard_map/ppermute | solution.py:451
  25.0 20.3 %collective-permute-start.137 = (bf16[448,128]{1,0:T(8,128)(2,1)S(1)}, bf16[448,128]{1,0:T(8,128)(2,1)S(1)}, u32[]{:S(2)}, u32[]{:S(2)}) collective-permute-start(bf16[448,128]{1,0:T(8,128)(2,1)S(1)} %get-tuple-element.252), channel_id=1, source_target_pairs={{0,13},{1,12},{2,15},{3,14},{4,9},{5,8},{6,11},{7,10},{8,5},{9,4},... | collective-permute-start | bytes 344072 | tf_op jit(solution)/shard_map/ppermute | solution.py:451
  28.5 16.9 %collective-permute-start.138 = (bf16[448,128]{1,0:T(8,128)(2,1)S(1)}, bf16[448,128]{1,0:T(8,128)(2,1)S(1)}, u32[]{:S(2)}, u32[]{:S(2)}) collective-permute-start(bf16[448,128]{1,0:T(8,128)(2,1)S(1)} %get-tuple-element.253), channel_id=1, source_target_pairs={{0,6},{1,7},{2,4},{3,5},{4,2},{5,3},{6,0},{7,1},{8,14},{9,15},{10,... | collective-permute-start | bytes 344072 | tf_op jit(solution)/shard_map/ppermute | solution.py:451
  31.0 14.4 %collective-permute-start.139 = (bf16[448,128]{1,0:T(8,128)(2,1)S(1)}, bf16[448,128]{1,0:T(8,128)(2,1)S(1)}, u32[]{:S(2)}, u32[]{:S(2)}) collective-permute-start(bf16[448,128]{1,0:T(8,128)(2,1)S(1)} %get-tuple-element.254), channel_id=1, source_target_pairs={{0,14},{1,15},{2,12},{3,13},{4,10},{5,11},{6,8},{7,9},{8,6},{9,7},... | collective-permute-start | bytes 344072 | tf_op jit(solution)/shard_map/ppermute | solution.py:451
  38.7 6.8 %collective-permute-start.140 = (bf16[448,128]{1,0:T(8,128)(2,1)S(1)}, bf16[448,128]{1,0:T(8,128)(2,1)S(1)}, u32[]{:S(2)}, u32[]{:S(2)}) collective-permute-start(bf16[448,128]{1,0:T(8,128)(2,1)S(1)} %get-tuple-element.255), channel_id=1, source_target_pairs={{0,7},{1,6},{2,5},{3,4},{4,3},{5,2},{6,1},{7,0},{8,15},{9,14},{10,... | collective-permute-start | bytes 344072 | tf_op jit(solution)/shard_map/ppermute | solution.py:451
  38.7 8.4 %collective-permute-start.141 = (bf16[448,128]{1,0:T(8,128)(2,1)S(1)}, bf16[448,128]{1,0:T(8,128)(2,1)S(1)}, u32[]{:S(2)}, u32[]{:S(2)}) collective-permute-start(bf16[448,128]{1,0:T(8,128)(2,1)S(1)} %get-tuple-element.256), channel_id=1, source_target_pairs={{0,15},{1,14},{2,13},{3,12},{4,11},{5,10},{6,9},{7,8},{8,7},{9,6},... | collective-permute-start | bytes 344072 | tf_op jit(solution)/shard_map/ppermute | solution.py:451
  50.8 8.3 %collective-permute-start.44 = (bf16[64,1024]{1,0:T(8,128)(2,1)S(1)}, bf16[64,1024]{1,0:T(8,128)(2,1)}, u32[]{:S(2)}, u32[]{:S(2)}) collective-permute-start(bf16[64,1024]{1,0:T(8,128)(2,1)S(1)} %get-tuple-element.391), channel_id=1, source_target_pairs={{0,15},{1,14},{2,13},{3,12},{4,11},{5,10},{6,9},{7,8},{8,7},{9,6},... | collective-permute-start | bytes 393224 | tf_op jit(solution)/shard_map/cond/branch_11_fun/ppermute | solution.py:451
  54.6 8.8 %collective-permute-start.46 = (bf16[64,1024]{1,0:T(8,128)(2,1)S(1)}, bf16[64,1024]{1,0:T(8,128)(2,1)}, u32[]{:S(2)}, u32[]{:S(2)}) collective-permute-start(bf16[64,1024]{1,0:T(8,128)(2,1)S(1)} %get-tuple-element.392), channel_id=1, source_target_pairs={{0,15},{1,14},{2,13},{3,12},{4,11},{5,10},{6,9},{7,8},{8,7},{9,6},... | collective-permute-start | bytes 393224 | tf_op jit(solution)/shard_map/cond/branch_11_fun/ppermute | solution.py:451
  59.2 6.9 %collective-permute-start.45 = (bf16[64,1024]{1,0:T(8,128)(2,1)}, bf16[64,1024]{1,0:T(8,128)(2,1)}, u32[]{:S(2)}, u32[]{:S(2)}) collective-permute-start(bf16[64,1024]{1,0:T(8,128)(2,1)} %collective-permute-done.44), channel_id=1, source_target_pairs={{0,3},{1,2},{2,1},{3,0},{4,7},{5,6},{6,5},{7,4},{8,11},{9,10},{10,... | collective-permute-start | bytes 393224 | tf_op jit(solution)/shard_map/cond/branch_11_fun/ppermute | solution.py:451
  63.4 6.0 %collective-permute-start.47 = (bf16[64,1024]{1,0:T(8,128)(2,1)}, bf16[64,1024]{1,0:T(8,128)(2,1)}, u32[]{:S(2)}, u32[]{:S(2)}) collective-permute-start(bf16[64,1024]{1,0:T(8,128)(2,1)} %collective-permute-done.46), channel_id=1, source_target_pairs={{0,3},{1,2},{2,1},{3,0},{4,7},{5,6},{6,5},{7,4},{8,11},{9,10},{10,... | collective-permute-start | bytes 393224 | tf_op jit(solution)/shard_map/cond/branch_11_fun/ppermute | solution.py:451

commit v2 on v1

--- a/solution.py
+++ b/solution.py
@@ -192,7 +192,7 @@
     slots = CH * W
     bins = table_ref.shape[1] // 2
     shift = capacity.bit_length() - 1
-    width = 256
+    width = 512
     depth = 512
     loads = [
         pltpu.make_async_copy(
@@ -326,7 +326,7 @@
     )(me, mask, *arrived, table)
 
 
-BLOCK = 64
+BLOCK = 32
 PIECE = 16
 
 

time: 80.5 us -> 80.5 us (level)
  no operation moved by 1% of the time
where the time goes in v2:
time: 80.5 us; the launch traced here: 80.2 us
  starting transfers between devices  38.1 us (47%)
  waiting for transfers between devices  20.6 us (26%)
  Pallas kernels  16.1 us (20%)
  between operations  2.77 us (3%)
  local copies, waits for them, and re-layouts  2.6 us (3%)
    ppermute x19, starting transfers between devices, swap(): lax.ppermute(block, 'blk', [(low, low ^ mask) for low in range(count)])  38.1 us
    ppermute x19, waiting for transfers between devices, swap(): lax.ppermute(block, 'blk', [(low, low ^ mask) for low in range(count)])  20.6 us
    pallas_call x1, Pallas kernels, correlate(): pl.pallas_call(correlate_kernel, in_specs=[pl.BlockSpec(memory_space=pltp...  10.3 us
    pallas_call x1, Pallas kernels, whiten(): pl.pallas_call(functools.partial(whiten_kernel, capacity, plans, places),...  3.42 us
    pallas_call x1, Pallas kernels, pack(): pl.pallas_call(functools.partial(pack_kernel, owners, capacity, plans), i...  2.33 us
  transfers between devices with their start and end apart: 19, of which 9 were waited for; matrix products, arithmetic and copies ran while one was open for 3% of the time, Pallas kernels for 0%

profile of v2, /device:TPU:0, one launch (start us, length us, event | category | flops | bytes accessed | tf_op | source)
XLA Modules:
  0.0 80.2 jit_solution(15170295413304343940)
XLA Ops:
  0.0 2.3 %pack.3 = (bf16[520,128]{1,0:T(8,128)(2,1)S(1)}, bf16[448,128]{1,0:T(8,128)(2,1)S(1)}, bf16[448,128]{1,0:T(8,128)(2,1)S(1)}, bf16[448,128]{1,0:T(8,128)(2,1)S(1)...) custom-call(s32[1]{0:T(128)} %bitcast.1.me_ref, ...), custom_call_target="tpu_custom_call" | custom-call | tf_op jit(solution)/shard_map/pack/pallas_call | solution.py:174
  2.3 4.1 %collective-permute-start.127 = (bf16[448,128]{1,0:T(8,128)(2,1)S(1)}, bf16[448,128]{1,0:T(8,128)(2,1)S(1)}, u32[]{:S(2)}, u32[]{:S(2)}) collective-permute-start(bf16[448,128]{1,0:T(8,128)(2,1)S(1)} %get-tuple-element.242), channel_id=1, source_target_pairs={{0,8},{1,9},{2,10},{3,11},{4,12},{5,13},{6,14},{7,15},{8,0},{9,1},... | collective-permute-start | bytes 344072 | tf_op jit(solution)/shard_map/ppermute | solution.py:451
  6.4 0.0 collective-permute-start.128
  6.4 0.2 collective-permute-start.129
  6.6 1.8 %collective-permute-start.130 = (bf16[448,128]{1,0:T(8,128)(2,1)S(1)}, bf16[448,128]{1,0:T(8,128)(2,1)S(1)}, u32[]{:S(2)}, u32[]{:S(2)}) collective-permute-start(bf16[448,128]{1,0:T(8,128)(2,1)S(1)} %get-tuple-element.245), channel_id=1, source_target_pairs={{0,2},{1,3},{2,0},{3,1},{4,6},{5,7},{6,4},{7,5},{8,10},{9,11},{10,... | collective-permute-start | bytes 344072 | tf_op jit(solution)/shard_map/ppermute | solution.py:451
  8.4 2.5 %collective-permute-start.131 = (bf16[448,128]{1,0:T(8,128)(2,1)S(1)}, bf16[448,128]{1,0:T(8,128)(2,1)S(1)}, u32[]{:S(2)}, u32[]{:S(2)}) collective-permute-start(bf16[448,128]{1,0:T(8,128)(2,1)S(1)} %get-tuple-element.246), channel_id=1, source_target_pairs={{0,10},{1,11},{2,8},{3,9},{4,14},{5,15},{6,12},{7,13},{8,2},{9,3},... | collective-permute-start | bytes 344072 | tf_op jit(solution)/shard_map/ppermute | solution.py:451
  10.9 6.8 %collective-permute-done.127.refs_0_ = bf16[448,128]{1,0:T(8,128)(2,1)S(1)} collective-permute-done((bf16[448,128]{1,0:T(8,128)(2,1)S(1)}, bf16[448,128]{1,0:T(8,128)(2,1)S(1)}, u32[]{:S(2)}, u32[]{:S(2)}) %collective-permute-start.127) | collective-permute-done | bytes 114720 | tf_op jit(solution)/shard_map/ppermute | solution.py:451
  17.8 0.0 collective-permute-start.132
  17.8 0.0 collective-permute-done.128.refs_1_
  17.8 0.7 collective-permute-start.133
  18.5 0.1 collective-permute-done.129.refs_2_
  18.6 3.8 %collective-permute-start.134 = (bf16[448,128]{1,0:T(8,128)(2,1)S(1)}, bf16[448,128]{1,0:T(8,128)(2,1)S(1)}, u32[]{:S(2)}, u32[]{:S(2)}) collective-permute-start(bf16[448,128]{1,0:T(8,128)(2,1)S(1)} %get-tuple-element.249), channel_id=1, source_target_pairs={{0,4},{1,5},{2,6},{3,7},{4,0},{5,1},{6,2},{7,3},{8,12},{9,13},{10,... | collective-permute-start | bytes 344072 | tf_op jit(solution)/shard_map/ppermute | solution.py:451
  22.3 0.0 collective-permute-done.130.refs_3_
  22.3 1.0 %collective-permute-start.135 = (bf16[448,128]{1,0:T(8,128)(2,1)S(1)}, bf16[448,128]{1,0:T(8,128)(2,1)S(1)}, u32[]{:S(2)}, u32[]{:S(2)}) collective-permute-start(bf16[448,128]{1,0:T(8,128)(2,1)S(1)} %get-tuple-element.250), channel_id=1, source_target_pairs={{0,12},{1,13},{2,14},{3,15},{4,8},{5,9},{6,10},{7,11},{8,4},{9,5},... | collective-permute-start | bytes 344072 | tf_op jit(solution)/shard_map/ppermute | solution.py:451
  23.3 0.0 collective-permute-done.131.refs_4_
  23.4 1.4 %collective-permute-start.136 = (bf16[448,128]{1,0:T(8,128)(2,1)S(1)}, bf16[448,128]{1,0:T(8,128)(2,1)S(1)}, u32[]{:S(2)}, u32[]{:S(2)}) collective-permute-start(bf16[448,128]{1,0:T(8,128)(2,1)S(1)} %get-tuple-element.251), channel_id=1, source_target_pairs={{0,5},{1,4},{2,7},{3,6},{4,1},{5,0},{6,3},{7,2},{8,13},{9,12},{10,... | collective-permute-start | bytes 344072 | tf_op jit(solution)/shard_map/ppermute | solution.py:451
  24.7 0.3 collective-permute-done.132.refs_5_
  25.0 3.5 %collective-permute-start.137 = (bf16[448,128]{1,0:T(8,128)(2,1)S(1)}, bf16[448,128]{1,0:T(8,128)(2,1)S(1)}, u32[]{:S(2)}, u32[]{:S(2)}) collective-permute-start(bf16[448,128]{1,0:T(8,128)(2,1)S(1)} %get-tuple-element.252), channel_id=1, source_target_pairs={{0,13},{1,12},{2,15},{3,14},{4,9},{5,8},{6,11},{7,10},{8,5},{9,4},... | collective-permute-start | bytes 344072 | tf_op jit(solution)/shard_map/ppermute | solution.py:451
  28.5 0.0 collective-permute-done.133.refs_6_
  28.5 2.5 %collective-permute-start.138 = (bf16[448,128]{1,0:T(8,128)(2,1)S(1)}, bf16[448,128]{1,0:T(8,128)(2,1)S(1)}, u32[]{:S(2)}, u32[]{:S(2)}) collective-permute-start(bf16[448,128]{1,0:T(8,128)(2,1)S(1)} %get-tuple-element.253), channel_id=1, source_target_pairs={{0,6},{1,7},{2,4},{3,5},{4,2},{5,3},{6,0},{7,1},{8,14},{9,15},{10,... | collective-permute-start | bytes 344072 | tf_op jit(solution)/shard_map/ppermute | solution.py:451
  31.0 0.0 collective-permute-done.134.refs_7_
  31.0 7.7 %collective-permute-start.139 = (bf16[448,128]{1,0:T(8,128)(2,1)S(1)}, bf16[448,128]{1,0:T(8,128)(2,1)S(1)}, u32[]{:S(2)}, u32[]{:S(2)}) collective-permute-start(bf16[448,128]{1,0:T(8,128)(2,1)S(1)} %get-tuple-element.254), channel_id=1, source_target_pairs={{0,14},{1,15},{2,12},{3,13},{4,10},{5,11},{6,8},{7,9},{8,6},{9,7},... | collective-permute-start | bytes 344072 | tf_op jit(solution)/shard_map/ppermute | solution.py:451
  38.7 0.0 collective-permute-done.135.refs_8_
  38.7 0.0 collective-permute-start.140
  38.7 0.0 collective-permute-done.136.refs_9_
  38.7 3.4 %collective-permute-start.141 = (bf16[448,128]{1,0:T(8,128)(2,1)S(1)}, bf16[448,128]{1,0:T(8,128)(2,1)S(1)}, u32[]{:S(2)}, u32[]{:S(2)}) collective-permute-start(bf16[448,128]{1,0:T(8,128)(2,1)S(1)} %get-tuple-element.256), channel_id=1, source_target_pairs={{0,15},{1,14},{2,13},{3,12},{4,11},{5,10},{6,9},{7,8},{8,7},{9,6},... | collective-permute-start | bytes 344072 | tf_op jit(solution)/shard_map/ppermute | solution.py:451
  42.1 1.3 %fusion = (s32[1]{0:T(128)}, s32[1]{0:T(128)}) fusion(s32[2]{0:T(128)} %param.42), kind=kLoop, calls=%fused_computation | loop fusion | bytes 16 | tf_op jit(solution)/shard_map/slice | solution.py:497
  45.3 0.0 collective-permute-done.137.refs_10_
  45.3 0.0 collective-permute-done.138.refs_11_
  45.3 0.0 collective-permute-done.139.refs_12_
  45.3 0.2 collective-permute-done.140.refs_13_
  45.5 1.6 %collective-permute-done.141.refs_14_ = bf16[448,128]{1,0:T(8,128)(2,1)S(1)} collective-permute-done((bf16[448,128]{1,0:T(8,128)(2,1)S(1)}, bf16[448,128]{1,0:T(8,128)(2,1)S(1)}, u32[]{:S(2)}, u32[]{:S(2)}) %collective-permute-start.141) | collective-permute-done | bytes 114720 | tf_op jit(solution)/shard_map/ppermute | solution.py:451
  47.1 3.4 %whiten.3 = (bf16[64,1024]{1,0:T(8,128)(2,1)S(1)}, bf16[64,1024]{1,0:T(8,128)(2,1)S(1)}, s32[1]{0:T(128)}) custom-call(s32[1]{0:T(128)} %bitcast.1.me_ref, s32[1]{0:T(128)} %sub.3.mask_ref, bf16[448,128]{1,0:T(8,128)(2,1)S(1)} %collective-permute-done.127.refs_0_, bf16[448,128]{1,0:T(8,128)(2,1)S(1)} %collective-permute-done.128.refs_1_, ...), custom_call_target="tpu_custom_call" | custom-call | tf_op jit(solution)/shard_map/whiten/pallas_call | solution.py:307
  51.2 18.6 %conditional.2 = (bf16[64,1024]{1,0:T(8,128)(2,1)}, bf16[64,1024]{1,0:T(8,128)(2,1)}, bf16[64,1024]{1,0:T(8,128)(2,1)}, bf16[64,1024]{1,0:T(8,128)(2,1)}, bf16[6...) conditional(s32[]{:T(128)} %bitcast.5, (bf16[64,1024]{1,0:T(8,128)(2,1)S(1)}, ...), branch_computations={%region_0.0_spmd, %region_1.0_spmd, %region_2.0_spmd, %region_3.0_... | conditional | flops 1 | bytes 10085224 | solution.py:507
  51.2 3.8 %collective-permute-start.44 = (bf16[64,1024]{1,0:T(8,128)(2,1)S(1)}, bf16[64,1024]{1,0:T(8,128)(2,1)}, u32[]{:S(2)}, u32[]{:S(2)}) collective-permute-start(bf16[64,1024]{1,0:T(8,128)(2,1)S(1)} %get-tuple-element.391), channel_id=1, source_target_pairs={{0,15},{1,14},{2,13},{3,12},{4,11},{5,10},{6,9},{7,8},{8,7},{9,6},... | collective-permute-start | bytes 393224 | tf_op jit(solution)/shard_map/cond/branch_11_fun/ppermute | solution.py:451
  55.0 0.8 collective-permute-start.46
  55.7 3.8 %collective-permute-done.44 = bf16[64,1024]{1,0:T(8,128)(2,1)} collective-permute-done((bf16[64,1024]{1,0:T(8,128)(2,1)S(1)}, bf16[64,1024]{1,0:T(8,128)(2,1)}, u32[]{:S(2)}, u32[]{:S(2)}) %collective-permute-start.44) | collective-permute-done | bytes 131104 | tf_op jit(solution)/shard_map/cond/branch_11_fun/ppermute | solution.py:451
  59.5 0.4 collective-permute-start.45
  59.9 3.9 %collective-permute-done.46 = bf16[64,1024]{1,0:T(8,128)(2,1)} collective-permute-done((bf16[64,1024]{1,0:T(8,128)(2,1)S(1)}, bf16[64,1024]{1,0:T(8,128)(2,1)}, u32[]{:S(2)}, u32[]{:S(2)}) %collective-permute-start.46) | collective-permute-done | bytes 131104 | tf_op jit(solution)/shard_map/cond/branch_11_fun/ppermute | solution.py:451
  63.8 0.7 collective-permute-start.47
  64.5 0.7 copy.132
  65.1 0.6 copy.133
  65.8 0.7 collective-permute-done.45
  66.4 3.3 %collective-permute-done.47 = bf16[64,1024]{1,0:T(8,128)(2,1)} collective-permute-done((bf16[64,1024]{1,0:T(8,128)(2,1)}, bf16[64,1024]{1,0:T(8,128)(2,1)}, u32[]{:S(2)}, u32[]{:S(2)}) %collective-permute-start.47) | collective-permute-done | bytes 131104 | tf_op jit(solution)/shard_map/cond/branch_11_fun/ppermute | solution.py:451
  69.7 10.3 %correlate.1 = bf16[2,128,128,128]{3,2,1,0:T(8,128)(2,1)} custom-call(s32[1]{0:T(128)S(6)} %convert_element_type.3.order_ref, bf16[64,1024]{1,0:T(8,128)(2,1)} %get-tuple-element.261.own_low, bf16[64,1024]{1,0:T(8,128)(2,1)} %get-tuple-element.262.own_high, bf16[96,256]{1,0:T(8,128)(2,1)} %constant.29.clone.rows_ref, ...), custom_call_target="tpu_custom_call" | custom-call | tf_op jit(solution)/shard_map/correlate/pallas_call | solution.py:425
Async XLA Ops:
  2.3 15.4 %collective-permute-start.127 = (bf16[448,128]{1,0:T(8,128)(2,1)S(1)}, bf16[448,128]{1,0:T(8,128)(2,1)S(1)}, u32[]{:S(2)}, u32[]{:S(2)}) collective-permute-start(bf16[448,128]{1,0:T(8,128)(2,1)S(1)} %get-tuple-element.242), channel_id=1, source_target_pairs={{0,8},{1,9},{2,10},{3,11},{4,12},{5,13},{6,14},{7,15},{8,0},{9,1},... | collective-permute-start | bytes 344072 | tf_op jit(solution)/shard_map/ppermute | solution.py:451
  6.4 11.4 %collective-permute-start.128 = (bf16[448,128]{1,0:T(8,128)(2,1)S(1)}, bf16[448,128]{1,0:T(8,128)(2,1)S(1)}, u32[]{:S(2)}, u32[]{:S(2)}) collective-permute-start(bf16[448,128]{1,0:T(8,128)(2,1)S(1)} %get-tuple-element.243), channel_id=1, source_target_pairs={{0,1},{1,0},{2,3},{3,2},{4,5},{5,4},{6,7},{7,6},{8,9},{9,8},{10,11... | collective-permute-start | bytes 344072 | tf_op jit(solution)/shard_map/ppermute | solution.py:451
  6.4 12.2 %collective-permute-start.129 = (bf16[448,128]{1,0:T(8,128)(2,1)S(1)}, bf16[448,128]{1,0:T(8,128)(2,1)S(1)}, u32[]{:S(2)}, u32[]{:S(2)}) collective-permute-start(bf16[448,128]{1,0:T(8,128)(2,1)S(1)} %get-tuple-element.244), channel_id=1, source_target_pairs={{0,9},{1,8},{2,11},{3,10},{4,13},{5,12},{6,15},{7,14},{8,1},{9,0},... | collective-permute-start | bytes 344072 | tf_op jit(solution)/shard_map/ppermute | solution.py:451
  6.6 15.7 %collective-permute-start.130 = (bf16[448,128]{1,0:T(8,128)(2,1)S(1)}, bf16[448,128]{1,0:T(8,128)(2,1)S(1)}, u32[]{:S(2)}, u32[]{:S(2)}) collective-permute-start(bf16[448,128]{1,0:T(8,128)(2,1)S(1)} %get-tuple-element.245), channel_id=1, source_target_pairs={{0,2},{1,3},{2,0},{3,1},{4,6},{5,7},{6,4},{7,5},{8,10},{9,11},{10,... | collective-permute-start | bytes 344072 | tf_op jit(solution)/shard_map/ppermute | solution.py:451
  8.4 14.9 %collective-permute-start.131 = (bf16[448,128]{1,0:T(8,128)(2,1)S(1)}, bf16[448,128]{1,0:T(8,128)(2,1)S(1)}, u32[]{:S(2)}, u32[]{:S(2)}) collective-permute-start(bf16[448,128]{1,0:T(8,128)(2,1)S(1)} %get-tuple-element.246), channel_id=1, source_target_pairs={{0,10},{1,11},{2,8},{3,9},{4,14},{5,15},{6,12},{7,13},{8,2},{9,3},... | collective-permute-start | bytes 344072 | tf_op jit(solution)/shard_map/ppermute | solution.py:451
  17.8 7.2 %collective-permute-start.132 = (bf16[448,128]{1,0:T(8,128)(2,1)S(1)}, bf16[448,128]{1,0:T(8,128)(2,1)S(1)}, u32[]{:S(2)}, u32[]{:S(2)}) collective-permute-start(bf16[448,128]{1,0:T(8,128)(2,1)S(1)} %get-tuple-element.247), channel_id=1, source_target_pairs={{0,3},{1,2},{2,1},{3,0},{4,7},{5,6},{6,5},{7,4},{8,11},{9,10},{10,... | collective-permute-start | bytes 344072 | tf_op jit(solution)/shard_map/ppermute | solution.py:451
  17.8 10.7 %collective-permute-start.133 = (bf16[448,128]{1,0:T(8,128)(2,1)S(1)}, bf16[448,128]{1,0:T(8,128)(2,1)S(1)}, u32[]{:S(2)}, u32[]{:S(2)}) collective-permute-start(bf16[448,128]{1,0:T(8,128)(2,1)S(1)} %get-tuple-element.248), channel_id=1, source_target_pairs={{0,11},{1,10},{2,9},{3,8},{4,15},{5,14},{6,13},{7,12},{8,3},{9,2},... | collective-permute-start | bytes 344072 | tf_op jit(solution)/shard_map/ppermute | solution.py:451
  18.6 12.4 %collective-permute-start.134 = (bf16[448,128]{1,0:T(8,128)(2,1)S(1)}, bf16[448,128]{1,0:T(8,128)(2,1)S(1)}, u32[]{:S(2)}, u32[]{:S(2)}) collective-permute-start(bf16[448,128]{1,0:T(8,128)(2,1)S(1)} %get-tuple-element.249), channel_id=1, source_target_pairs={{0,4},{1,5},{2,6},{3,7},{4,0},{5,1},{6,2},{7,3},{8,12},{9,13},{10,... | collective-permute-start | bytes 344072 | tf_op jit(solution)/shard_map/ppermute | solution.py:451
  22.3 16.4 %collective-permute-start.135 = (bf16[448,128]{1,0:T(8,128)(2,1)S(1)}, bf16[448,128]{1,0:T(8,128)(2,1)S(1)}, u32[]{:S(2)}, u32[]{:S(2)}) collective-permute-start(bf16[448,128]{1,0:T(8,128)(2,1)S(1)} %get-tuple-element.250), channel_id=1, source_target_pairs={{0,12},{1,13},{2,14},{3,15},{4,8},{5,9},{6,10},{7,11},{8,4},{9,5},... | collective-permute-start | bytes 344072 | tf_op jit(solution)/shard_map/ppermute | solution.py:451
  23.4 15.3 %collective-permute-start.136 = (bf16[448,128]{1,0:T(8,128)(2,1)S(1)}, bf16[448,128]{1,0:T(8,128)(2,1)S(1)}, u32[]{:S(2)}, u32[]{:S(2)}) collective-permute-start(bf16[448,128]{1,0:T(8,128)(2,1)S(1)} %get-tuple-element.251), channel_id=1, source_target_pairs={{0,5},{1,4},{2,7},{3,6},{4,1},{5,0},{6,3},{7,2},{8,13},{9,12},{10,... | collective-permute-start | bytes 344072 | tf_op jit(solution)/shard_map/ppermute | solution.py:451
  25.0 20.3 %collective-permute-start.137 = (bf16[448,128]{1,0:T(8,128)(2,1)S(1)}, bf16[448,128]{1,0:T(8,128)(2,1)S(1)}, u32[]{:S(2)}, u32[]{:S(2)}) collective-permute-start(bf16[448,128]{1,0:T(8,128)(2,1)S(1)} %get-tuple-element.252), channel_id=1, source_target_pairs={{0,13},{1,12},{2,15},{3,14},{4,9},{5,8},{6,11},{7,10},{8,5},{9,4},... | collective-permute-start | bytes 344072 | tf_op jit(solution)/shard_map/ppermute | solution.py:451
  28.5 16.9 %collective-permute-start.138 = (bf16[448,128]{1,0:T(8,128)(2,1)S(1)}, bf16[448,128]{1,0:T(8,128)(2,1)S(1)}, u32[]{:S(2)}, u32[]{:S(2)}) collective-permute-start(bf16[448,128]{1,0:T(8,128)(2,1)S(1)} %get-tuple-element.253), channel_id=1, source_target_pairs={{0,6},{1,7},{2,4},{3,5},{4,2},{5,3},{6,0},{7,1},{8,14},{9,15},{10,... | collective-permute-start | bytes 344072 | tf_op jit(solution)/shard_map/ppermute | solution.py:451
  31.0 14.4 %collective-permute-start.139 = (bf16[448,128]{1,0:T(8,128)(2,1)S(1)}, bf16[448,128]{1,0:T(8,128)(2,1)S(1)}, u32[]{:S(2)}, u32[]{:S(2)}) collective-permute-start(bf16[448,128]{1,0:T(8,128)(2,1)S(1)} %get-tuple-element.254), channel_id=1, source_target_pairs={{0,14},{1,15},{2,12},{3,13},{4,10},{5,11},{6,8},{7,9},{8,6},{9,7},... | collective-permute-start | bytes 344072 | tf_op jit(solution)/shard_map/ppermute | solution.py:451
  38.7 6.8 %collective-permute-start.140 = (bf16[448,128]{1,0:T(8,128)(2,1)S(1)}, bf16[448,128]{1,0:T(8,128)(2,1)S(1)}, u32[]{:S(2)}, u32[]{:S(2)}) collective-permute-start(bf16[448,128]{1,0:T(8,128)(2,1)S(1)} %get-tuple-element.255), channel_id=1, source_target_pairs={{0,7},{1,6},{2,5},{3,4},{4,3},{5,2},{6,1},{7,0},{8,15},{9,14},{10,... | collective-permute-start | bytes 344072 | tf_op jit(solution)/shard_map/ppermute | solution.py:451
  38.7 8.4 %collective-permute-start.141 = (bf16[448,128]{1,0:T(8,128)(2,1)S(1)}, bf16[448,128]{1,0:T(8,128)(2,1)S(1)}, u32[]{:S(2)}, u32[]{:S(2)}) collective-permute-start(bf16[448,128]{1,0:T(8,128)(2,1)S(1)} %get-tuple-element.256), channel_id=1, source_target_pairs={{0,15},{1,14},{2,13},{3,12},{4,11},{5,10},{6,9},{7,8},{8,7},{9,6},... | collective-permute-start | bytes 344072 | tf_op jit(solution)/shard_map/ppermute | solution.py:451
  51.2 8.3 %collective-permute-start.44 = (bf16[64,1024]{1,0:T(8,128)(2,1)S(1)}, bf16[64,1024]{1,0:T(8,128)(2,1)}, u32[]{:S(2)}, u32[]{:S(2)}) collective-permute-start(bf16[64,1024]{1,0:T(8,128)(2,1)S(1)} %get-tuple-element.391), channel_id=1, source_target_pairs={{0,15},{1,14},{2,13},{3,12},{4,11},{5,10},{6,9},{7,8},{8,7},{9,6},... | collective-permute-start | bytes 393224 | tf_op jit(solution)/shard_map/cond/branch_11_fun/ppermute | solution.py:451
  55.0 8.8 %collective-permute-start.46 = (bf16[64,1024]{1,0:T(8,128)(2,1)S(1)}, bf16[64,1024]{1,0:T(8,128)(2,1)}, u32[]{:S(2)}, u32[]{:S(2)}) collective-permute-start(bf16[64,1024]{1,0:T(8,128)(2,1)S(1)} %get-tuple-element.392), channel_id=1, source_target_pairs={{0,15},{1,14},{2,13},{3,12},{4,11},{5,10},{6,9},{7,8},{8,7},{9,6},... | collective-permute-start | bytes 393224 | tf_op jit(solution)/shard_map/cond/branch_11_fun/ppermute | solution.py:451
  59.5 6.9 %collective-permute-start.45 = (bf16[64,1024]{1,0:T(8,128)(2,1)}, bf16[64,1024]{1,0:T(8,128)(2,1)}, u32[]{:S(2)}, u32[]{:S(2)}) collective-permute-start(bf16[64,1024]{1,0:T(8,128)(2,1)} %collective-permute-done.44), channel_id=1, source_target_pairs={{0,3},{1,2},{2,1},{3,0},{4,7},{5,6},{6,5},{7,4},{8,11},{9,10},{10,... | collective-permute-start | bytes 393224 | tf_op jit(solution)/shard_map/cond/branch_11_fun/ppermute | solution.py:451
  63.8 6.0 %collective-permute-start.47 = (bf16[64,1024]{1,0:T(8,128)(2,1)}, bf16[64,1024]{1,0:T(8,128)(2,1)}, u32[]{:S(2)}, u32[]{:S(2)}) collective-permute-start(bf16[64,1024]{1,0:T(8,128)(2,1)} %collective-permute-done.46), channel_id=1, source_target_pairs={{0,3},{1,2},{2,1},{3,0},{4,7},{5,6},{6,5},{7,4},{8,11},{9,10},{10,... | collective-permute-start | bytes 393224 | tf_op jit(solution)/shard_map/cond/branch_11_fun/ppermute | solution.py:451

commit v3 on v2

--- a/solution.py
+++ b/solution.py
@@ -192,7 +192,7 @@
     slots = CH * W
     bins = table_ref.shape[1] // 2
     shift = capacity.bit_length() - 1
-    width = 512
+    width = 256
     depth = 512
     loads = [
         pltpu.make_async_copy(
@@ -327,7 +327,7 @@
 
 
 BLOCK = 32
-PIECE = 16
+PIECE = 32
 
 
 def correlate_kernel(

time: 80.5 us -> 80.6 us (level)
  starting transfers between devices: 38.1 us -> 43.4 us
  waiting for transfers between devices: 20.6 us -> 15.6 us
    ppermute x19, starting transfers between devices: 38.1 us -> 43.4 us  [swap(): lax.ppermute(block, 'blk', [(low, low ^ mask) for low in range(count)])]
    ppermute x19, waiting for transfers between devices: 20.6 us -> 15.6 us  [swap(): lax.ppermute(block, 'blk', [(low, low ^ mask) for low in range(count)])]
  transfers between devices with their start and end apart: 19 -> 19, of which waited for: 9 -> 8; matrix products, arithmetic and copies ran while one was open for 3% -> 3% of each run, Pallas kernels for 0% -> 0%
where the time goes in v3:
time: 80.6 us; the launch traced here: 80.5 us
  starting transfers between devices  43.4 us (54%)
  Pallas kernels  16 us (20%)
  waiting for transfers between devices  15.6 us (19%)
  between operations  2.77 us (3%)
  local copies, waits for them, and re-layouts  2.6 us (3%)
    ppermute x19, starting transfers between devices, swap(): lax.ppermute(block, 'blk', [(low, low ^ mask) for low in range(count)])  43.4 us
    ppermute x19, waiting for transfers between devices, swap(): lax.ppermute(block, 'blk', [(low, low ^ mask) for low in range(count)])  15.6 us
    pallas_call x1, Pallas kernels, correlate(): pl.pallas_call(correlate_kernel, in_specs=[pl.BlockSpec(memory_space=pltp...  10.6 us
    pallas_call x1, Pallas kernels, whiten(): pl.pallas_call(functools.partial(whiten_kernel, capacity, plans, places),...  3.05 us
    pallas_call x1, Pallas kernels, pack(): pl.pallas_call(functools.partial(pack_kernel, owners, capacity, plans), i...  2.33 us
  transfers between devices with their start and end apart: 19, of which 8 were waited for; matrix products, arithmetic and copies ran while one was open for 3% of the time, Pallas kernels for 0%

profile of v3, /device:TPU:0, one launch (start us, length us, event | category | flops | bytes accessed | tf_op | source)
XLA Modules:
  0.0 80.5 jit_solution(15706000605278318841)
XLA Ops:
  0.0 2.3 %pack.3 = (bf16[520,128]{1,0:T(8,128)(2,1)S(1)}, bf16[448,128]{1,0:T(8,128)(2,1)S(1)}, bf16[448,128]{1,0:T(8,128)(2,1)S(1)}, bf16[448,128]{1,0:T(8,128)(2,1)S(1)...) custom-call(s32[1]{0:T(128)} %bitcast.1.me_ref, ...), custom_call_target="tpu_custom_call" | custom-call | tf_op jit(solution)/shard_map/pack/pallas_call | solution.py:174
  2.3 4.1 %collective-permute-start.127 = (bf16[448,128]{1,0:T(8,128)(2,1)S(1)}, bf16[448,128]{1,0:T(8,128)(2,1)S(1)}, u32[]{:S(2)}, u32[]{:S(2)}) collective-permute-start(bf16[448,128]{1,0:T(8,128)(2,1)S(1)} %get-tuple-element.242), channel_id=1, source_target_pairs={{0,8},{1,9},{2,10},{3,11},{4,12},{5,13},{6,14},{7,15},{8,0},{9,1},... | collective-permute-start | bytes 344072 | tf_op jit(solution)/shard_map/ppermute | solution.py:451
  6.4 0.0 collective-permute-start.128
  6.4 0.2 collective-permute-start.129
  6.6 1.8 %collective-permute-start.130 = (bf16[448,128]{1,0:T(8,128)(2,1)S(1)}, bf16[448,128]{1,0:T(8,128)(2,1)S(1)}, u32[]{:S(2)}, u32[]{:S(2)}) collective-permute-start(bf16[448,128]{1,0:T(8,128)(2,1)S(1)} %get-tuple-element.245), channel_id=1, source_target_pairs={{0,2},{1,3},{2,0},{3,1},{4,6},{5,7},{6,4},{7,5},{8,10},{9,11},{10,... | collective-permute-start | bytes 344072 | tf_op jit(solution)/shard_map/ppermute | solution.py:451
  8.4 2.5 %collective-permute-start.131 = (bf16[448,128]{1,0:T(8,128)(2,1)S(1)}, bf16[448,128]{1,0:T(8,128)(2,1)S(1)}, u32[]{:S(2)}, u32[]{:S(2)}) collective-permute-start(bf16[448,128]{1,0:T(8,128)(2,1)S(1)} %get-tuple-element.246), channel_id=1, source_target_pairs={{0,10},{1,11},{2,8},{3,9},{4,14},{5,15},{6,12},{7,13},{8,2},{9,3},... | collective-permute-start | bytes 344072 | tf_op jit(solution)/shard_map/ppermute | solution.py:451
  10.9 6.8 %collective-permute-done.127.refs_0_ = bf16[448,128]{1,0:T(8,128)(2,1)S(1)} collective-permute-done((bf16[448,128]{1,0:T(8,128)(2,1)S(1)}, bf16[448,128]{1,0:T(8,128)(2,1)S(1)}, u32[]{:S(2)}, u32[]{:S(2)}) %collective-permute-start.127) | collective-permute-done | bytes 114720 | tf_op jit(solution)/shard_map/ppermute | solution.py:451
  17.8 0.0 collective-permute-start.132
  17.8 0.0 collective-permute-done.128.refs_1_
  17.8 0.7 collective-permute-start.133
  18.5 0.1 collective-permute-done.129.refs_2_
  18.6 3.8 %collective-permute-start.134 = (bf16[448,128]{1,0:T(8,128)(2,1)S(1)}, bf16[448,128]{1,0:T(8,128)(2,1)S(1)}, u32[]{:S(2)}, u32[]{:S(2)}) collective-permute-start(bf16[448,128]{1,0:T(8,128)(2,1)S(1)} %get-tuple-element.249), channel_id=1, source_target_pairs={{0,4},{1,5},{2,6},{3,7},{4,0},{5,1},{6,2},{7,3},{8,12},{9,13},{10,... | collective-permute-start | bytes 344072 | tf_op jit(solution)/shard_map/ppermute | solution.py:451
  22.3 0.0 collective-permute-done.130.refs_3_
  22.3 1.0 %collective-permute-start.135 = (bf16[448,128]{1,0:T(8,128)(2,1)S(1)}, bf16[448,128]{1,0:T(8,128)(2,1)S(1)}, u32[]{:S(2)}, u32[]{:S(2)}) collective-permute-start(bf16[448,128]{1,0:T(8,128)(2,1)S(1)} %get-tuple-element.250), channel_id=1, source_target_pairs={{0,12},{1,13},{2,14},{3,15},{4,8},{5,9},{6,10},{7,11},{8,4},{9,5},... | collective-permute-start | bytes 344072 | tf_op jit(solution)/shard_map/ppermute | solution.py:451
  23.3 0.0 collective-permute-done.131.refs_4_
  23.4 1.4 %collective-permute-start.136 = (bf16[448,128]{1,0:T(8,128)(2,1)S(1)}, bf16[448,128]{1,0:T(8,128)(2,1)S(1)}, u32[]{:S(2)}, u32[]{:S(2)}) collective-permute-start(bf16[448,128]{1,0:T(8,128)(2,1)S(1)} %get-tuple-element.251), channel_id=1, source_target_pairs={{0,5},{1,4},{2,7},{3,6},{4,1},{5,0},{6,3},{7,2},{8,13},{9,12},{10,... | collective-permute-start | bytes 344072 | tf_op jit(solution)/shard_map/ppermute | solution.py:451
  24.7 0.3 collective-permute-done.132.refs_5_
  25.0 3.5 %collective-permute-start.137 = (bf16[448,128]{1,0:T(8,128)(2,1)S(1)}, bf16[448,128]{1,0:T(8,128)(2,1)S(1)}, u32[]{:S(2)}, u32[]{:S(2)}) collective-permute-start(bf16[448,128]{1,0:T(8,128)(2,1)S(1)} %get-tuple-element.252), channel_id=1, source_target_pairs={{0,13},{1,12},{2,15},{3,14},{4,9},{5,8},{6,11},{7,10},{8,5},{9,4},... | collective-permute-start | bytes 344072 | tf_op jit(solution)/shard_map/ppermute | solution.py:451
  28.5 0.0 collective-permute-done.133.refs_6_
  28.5 2.5 %collective-permute-start.138 = (bf16[448,128]{1,0:T(8,128)(2,1)S(1)}, bf16[448,128]{1,0:T(8,128)(2,1)S(1)}, u32[]{:S(2)}, u32[]{:S(2)}) collective-permute-start(bf16[448,128]{1,0:T(8,128)(2,1)S(1)} %get-tuple-element.253), channel_id=1, source_target_pairs={{0,6},{1,7},{2,4},{3,5},{4,2},{5,3},{6,0},{7,1},{8,14},{9,15},{10,... | collective-permute-start | bytes 344072 | tf_op jit(solution)/shard_map/ppermute | solution.py:451
  31.0 0.0 collective-permute-done.134.refs_7_
  31.0 7.7 %collective-permute-start.139 = (bf16[448,128]{1,0:T(8,128)(2,1)S(1)}, bf16[448,128]{1,0:T(8,128)(2,1)S(1)}, u32[]{:S(2)}, u32[]{:S(2)}) collective-permute-start(bf16[448,128]{1,0:T(8,128)(2,1)S(1)} %get-tuple-element.254), channel_id=1, source_target_pairs={{0,14},{1,15},{2,12},{3,13},{4,10},{5,11},{6,8},{7,9},{8,6},{9,7},... | collective-permute-start | bytes 344072 | tf_op jit(solution)/shard_map/ppermute | solution.py:451
  38.7 0.0 collective-permute-done.135.refs_8_
  38.7 0.0 collective-permute-start.140
  38.7 0.0 collective-permute-done.136.refs_9_
  38.7 3.4 %collective-permute-start.141 = (bf16[448,128]{1,0:T(8,128)(2,1)S(1)}, bf16[448,128]{1,0:T(8,128)(2,1)S(1)}, u32[]{:S(2)}, u32[]{:S(2)}) collective-permute-start(bf16[448,128]{1,0:T(8,128)(2,1)S(1)} %get-tuple-element.256), channel_id=1, source_target_pairs={{0,15},{1,14},{2,13},{3,12},{4,11},{5,10},{6,9},{7,8},{8,7},{9,6},... | collective-permute-start | bytes 344072 | tf_op jit(solution)/shard_map/ppermute | solution.py:451
  42.1 1.3 %fusion = (s32[1]{0:T(128)}, s32[1]{0:T(128)}) fusion(s32[2]{0:T(128)} %param.42), kind=kLoop, calls=%fused_computation | loop fusion | bytes 16 | tf_op jit(solution)/shard_map/slice | solution.py:497
  45.3 0.0 collective-permute-done.137.refs_10_
  45.3 0.0 collective-permute-done.138.refs_11_
  45.3 0.0 collective-permute-done.139.refs_12_
  45.3 0.2 collective-permute-done.140.refs_13_
  45.5 1.6 %collective-permute-done.141.refs_14_ = bf16[448,128]{1,0:T(8,128)(2,1)S(1)} collective-permute-done((bf16[448,128]{1,0:T(8,128)(2,1)S(1)}, bf16[448,128]{1,0:T(8,128)(2,1)S(1)}, u32[]{:S(2)}, u32[]{:S(2)}) %collective-permute-start.141) | collective-permute-done | bytes 114720 | tf_op jit(solution)/shard_map/ppermute | solution.py:451
  47.1 3.1 %whiten.3 = (bf16[64,1024]{1,0:T(8,128)(2,1)S(1)}, bf16[64,1024]{1,0:T(8,128)(2,1)S(1)}, s32[1]{0:T(128)}) custom-call(s32[1]{0:T(128)} %bitcast.1.me_ref, s32[1]{0:T(128)} %sub.3.mask_ref, bf16[448,128]{1,0:T(8,128)(2,1)S(1)} %collective-permute-done.127.refs_0_, bf16[448,128]{1,0:T(8,128)(2,1)S(1)} %collective-permute-done.128.refs_1_, ...), custom_call_target="tpu_custom_call" | custom-call | tf_op jit(solution)/shard_map/whiten/pallas_call | solution.py:307
  50.8 18.9 %conditional.2 = (bf16[64,1024]{1,0:T(8,128)(2,1)}, bf16[64,1024]{1,0:T(8,128)(2,1)}, bf16[64,1024]{1,0:T(8,128)(2,1)}, bf16[64,1024]{1,0:T(8,128)(2,1)}, bf16[6...) conditional(s32[]{:T(128)} %bitcast.5, (bf16[64,1024]{1,0:T(8,128)(2,1)S(1)}, ...), branch_computations={%region_0.0_spmd, %region_1.0_spmd, %region_2.0_spmd, %region_3.0_... | conditional | flops 1 | bytes 10085224 | solution.py:507
  50.8 3.8 %collective-permute-start.36 = (bf16[64,1024]{1,0:T(8,128)(2,1)S(1)}, bf16[64,1024]{1,0:T(8,128)(2,1)}, u32[]{:S(2)}, u32[]{:S(2)}) collective-permute-start(bf16[64,1024]{1,0:T(8,128)(2,1)S(1)} %get-tuple-element.379), channel_id=1, source_target_pairs={{0,15},{1,14},{2,13},{3,12},{4,11},{5,10},{6,9},{7,8},{8,7},{9,6},... | collective-permute-start | bytes 393224 | tf_op jit(solution)/shard_map/cond/branch_9_fun/ppermute | solution.py:451
  54.6 0.8 collective-permute-start.38
  55.4 3.8 %collective-permute-done.36 = bf16[64,1024]{1,0:T(8,128)(2,1)} collective-permute-done((bf16[64,1024]{1,0:T(8,128)(2,1)S(1)}, bf16[64,1024]{1,0:T(8,128)(2,1)}, u32[]{:S(2)}, u32[]{:S(2)}) %collective-permute-start.36) | collective-permute-done | bytes 131104 | tf_op jit(solution)/shard_map/cond/branch_9_fun/ppermute | solution.py:451
  59.2 4.5 %collective-permute-start.37 = (bf16[64,1024]{1,0:T(8,128)(2,1)}, bf16[64,1024]{1,0:T(8,128)(2,1)}, u32[]{:S(2)}, u32[]{:S(2)}) collective-permute-start(bf16[64,1024]{1,0:T(8,128)(2,1)} %collective-permute-done.36), channel_id=1, source_target_pairs={{0,5},{1,4},{2,7},{3,6},{4,1},{5,0},{6,3},{7,2},{8,13},{9,12},{10,... | collective-permute-start | bytes 393224 | tf_op jit(solution)/shard_map/cond/branch_9_fun/ppermute | solution.py:451
  63.6 0.0 collective-permute-done.38
  63.6 1.9 %collective-permute-start.39 = (bf16[64,1024]{1,0:T(8,128)(2,1)}, bf16[64,1024]{1,0:T(8,128)(2,1)}, u32[]{:S(2)}, u32[]{:S(2)}) collective-permute-start(bf16[64,1024]{1,0:T(8,128)(2,1)} %collective-permute-done.38), channel_id=1, source_target_pairs={{0,5},{1,4},{2,7},{3,6},{4,1},{5,0},{6,3},{7,2},{8,13},{9,12},{10,... | collective-permute-start | bytes 393224 | tf_op jit(solution)/shard_map/cond/branch_9_fun/ppermute | solution.py:451
  65.5 0.7 copy.120
  66.2 0.6 copy.121
  66.8 0.3 collective-permute-done.37
  67.1 2.6 %collective-permute-done.39 = bf16[64,1024]{1,0:T(8,128)(2,1)} collective-permute-done((bf16[64,1024]{1,0:T(8,128)(2,1)}, bf16[64,1024]{1,0:T(8,128)(2,1)}, u32[]{:S(2)}, u32[]{:S(2)}) %collective-permute-start.39) | collective-permute-done | bytes 131104 | tf_op jit(solution)/shard_map/cond/branch_9_fun/ppermute | solution.py:451
  69.7 10.6 %correlate.1 = bf16[2,128,128,128]{3,2,1,0:T(8,128)(2,1)} custom-call(s32[1]{0:T(128)S(6)} %convert_element_type.3.order_ref, bf16[64,1024]{1,0:T(8,128)(2,1)} %get-tuple-element.261.own_low, bf16[64,1024]{1,0:T(8,128)(2,1)} %get-tuple-element.262.own_high, bf16[96,256]{1,0:T(8,128)(2,1)} %constant.29.clone.rows_ref, ...), custom_call_target="tpu_custom_call" | custom-call | tf_op jit(solution)/shard_map/correlate/pallas_call | solution.py:425
Async XLA Ops:
  2.3 15.4 %collective-permute-start.127 = (bf16[448,128]{1,0:T(8,128)(2,1)S(1)}, bf16[448,128]{1,0:T(8,128)(2,1)S(1)}, u32[]{:S(2)}, u32[]{:S(2)}) collective-permute-start(bf16[448,128]{1,0:T(8,128)(2,1)S(1)} %get-tuple-element.242), channel_id=1, source_target_pairs={{0,8},{1,9},{2,10},{3,11},{4,12},{5,13},{6,14},{7,15},{8,0},{9,1},... | collective-permute-start | bytes 344072 | tf_op jit(solution)/shard_map/ppermute | solution.py:451
  6.4 11.4 %collective-permute-start.128 = (bf16[448,128]{1,0:T(8,128)(2,1)S(1)}, bf16[448,128]{1,0:T(8,128)(2,1)S(1)}, u32[]{:S(2)}, u32[]{:S(2)}) collective-permute-start(bf16[448,128]{1,0:T(8,128)(2,1)S(1)} %get-tuple-element.243), channel_id=1, source_target_pairs={{0,1},{1,0},{2,3},{3,2},{4,5},{5,4},{6,7},{7,6},{8,9},{9,8},{10,11... | collective-permute-start | bytes 344072 | tf_op jit(solution)/shard_map/ppermute | solution.py:451
  6.4 12.2 %collective-permute-start.129 = (bf16[448,128]{1,0:T(8,128)(2,1)S(1)}, bf16[448,128]{1,0:T(8,128)(2,1)S(1)}, u32[]{:S(2)}, u32[]{:S(2)}) collective-permute-start(bf16[448,128]{1,0:T(8,128)(2,1)S(1)} %get-tuple-element.244), channel_id=1, source_target_pairs={{0,9},{1,8},{2,11},{3,10},{4,13},{5,12},{6,15},{7,14},{8,1},{9,0},... | collective-permute-start | bytes 344072 | tf_op jit(solution)/shard_map/ppermute | solution.py:451
  6.6 15.7 %collective-permute-start.130 = (bf16[448,128]{1,0:T(8,128)(2,1)S(1)}, bf16[448,128]{1,0:T(8,128)(2,1)S(1)}, u32[]{:S(2)}, u32[]{:S(2)}) collective-permute-start(bf16[448,128]{1,0:T(8,128)(2,1)S(1)} %get-tuple-element.245), channel_id=1, source_target_pairs={{0,2},{1,3},{2,0},{3,1},{4,6},{5,7},{6,4},{7,5},{8,10},{9,11},{10,... | collective-permute-start | bytes 344072 | tf_op jit(solution)/shard_map/ppermute | solution.py:451
  8.4 14.9 %collective-permute-start.131 = (bf16[448,128]{1,0:T(8,128)(2,1)S(1)}, bf16[448,128]{1,0:T(8,128)(2,1)S(1)}, u32[]{:S(2)}, u32[]{:S(2)}) collective-permute-start(bf16[448,128]{1,0:T(8,128)(2,1)S(1)} %get-tuple-element.246), channel_id=1, source_target_pairs={{0,10},{1,11},{2,8},{3,9},{4,14},{5,15},{6,12},{7,13},{8,2},{9,3},... | collective-permute-start | bytes 344072 | tf_op jit(solution)/shard_map/ppermute | solution.py:451
  17.8 7.2 %collective-permute-start.132 = (bf16[448,128]{1,0:T(8,128)(2,1)S(1)}, bf16[448,128]{1,0:T(8,128)(2,1)S(1)}, u32[]{:S(2)}, u32[]{:S(2)}) collective-permute-start(bf16[448,128]{1,0:T(8,128)(2,1)S(1)} %get-tuple-element.247), channel_id=1, source_target_pairs={{0,3},{1,2},{2,1},{3,0},{4,7},{5,6},{6,5},{7,4},{8,11},{9,10},{10,... | collective-permute-start | bytes 344072 | tf_op jit(solution)/shard_map/ppermute | solution.py:451
  17.8 10.7 %collective-permute-start.133 = (bf16[448,128]{1,0:T(8,128)(2,1)S(1)}, bf16[448,128]{1,0:T(8,128)(2,1)S(1)}, u32[]{:S(2)}, u32[]{:S(2)}) collective-permute-start(bf16[448,128]{1,0:T(8,128)(2,1)S(1)} %get-tuple-element.248), channel_id=1, source_target_pairs={{0,11},{1,10},{2,9},{3,8},{4,15},{5,14},{6,13},{7,12},{8,3},{9,2},... | collective-permute-start | bytes 344072 | tf_op jit(solution)/shard_map/ppermute | solution.py:451
  18.6 12.4 %collective-permute-start.134 = (bf16[448,128]{1,0:T(8,128)(2,1)S(1)}, bf16[448,128]{1,0:T(8,128)(2,1)S(1)}, u32[]{:S(2)}, u32[]{:S(2)}) collective-permute-start(bf16[448,128]{1,0:T(8,128)(2,1)S(1)} %get-tuple-element.249), channel_id=1, source_target_pairs={{0,4},{1,5},{2,6},{3,7},{4,0},{5,1},{6,2},{7,3},{8,12},{9,13},{10,... | collective-permute-start | bytes 344072 | tf_op jit(solution)/shard_map/ppermute | solution.py:451
  22.3 16.4 %collective-permute-start.135 = (bf16[448,128]{1,0:T(8,128)(2,1)S(1)}, bf16[448,128]{1,0:T(8,128)(2,1)S(1)}, u32[]{:S(2)}, u32[]{:S(2)}) collective-permute-start(bf16[448,128]{1,0:T(8,128)(2,1)S(1)} %get-tuple-element.250), channel_id=1, source_target_pairs={{0,12},{1,13},{2,14},{3,15},{4,8},{5,9},{6,10},{7,11},{8,4},{9,5},... | collective-permute-start | bytes 344072 | tf_op jit(solution)/shard_map/ppermute | solution.py:451
  23.4 15.3 %collective-permute-start.136 = (bf16[448,128]{1,0:T(8,128)(2,1)S(1)}, bf16[448,128]{1,0:T(8,128)(2,1)S(1)}, u32[]{:S(2)}, u32[]{:S(2)}) collective-permute-start(bf16[448,128]{1,0:T(8,128)(2,1)S(1)} %get-tuple-element.251), channel_id=1, source_target_pairs={{0,5},{1,4},{2,7},{3,6},{4,1},{5,0},{6,3},{7,2},{8,13},{9,12},{10,... | collective-permute-start | bytes 344072 | tf_op jit(solution)/shard_map/ppermute | solution.py:451
  25.0 20.3 %collective-permute-start.137 = (bf16[448,128]{1,0:T(8,128)(2,1)S(1)}, bf16[448,128]{1,0:T(8,128)(2,1)S(1)}, u32[]{:S(2)}, u32[]{:S(2)}) collective-permute-start(bf16[448,128]{1,0:T(8,128)(2,1)S(1)} %get-tuple-element.252), channel_id=1, source_target_pairs={{0,13},{1,12},{2,15},{3,14},{4,9},{5,8},{6,11},{7,10},{8,5},{9,4},... | collective-permute-start | bytes 344072 | tf_op jit(solution)/shard_map/ppermute | solution.py:451
  28.5 16.9 %collective-permute-start.138 = (bf16[448,128]{1,0:T(8,128)(2,1)S(1)}, bf16[448,128]{1,0:T(8,128)(2,1)S(1)}, u32[]{:S(2)}, u32[]{:S(2)}) collective-permute-start(bf16[448,128]{1,0:T(8,128)(2,1)S(1)} %get-tuple-element.253), channel_id=1, source_target_pairs={{0,6},{1,7},{2,4},{3,5},{4,2},{5,3},{6,0},{7,1},{8,14},{9,15},{10,... | collective-permute-start | bytes 344072 | tf_op jit(solution)/shard_map/ppermute | solution.py:451
  31.0 14.4 %collective-permute-start.139 = (bf16[448,128]{1,0:T(8,128)(2,1)S(1)}, bf16[448,128]{1,0:T(8,128)(2,1)S(1)}, u32[]{:S(2)}, u32[]{:S(2)}) collective-permute-start(bf16[448,128]{1,0:T(8,128)(2,1)S(1)} %get-tuple-element.254), channel_id=1, source_target_pairs={{0,14},{1,15},{2,12},{3,13},{4,10},{5,11},{6,8},{7,9},{8,6},{9,7},... | collective-permute-start | bytes 344072 | tf_op jit(solution)/shard_map/ppermute | solution.py:451
  38.7 6.8 %collective-permute-start.140 = (bf16[448,128]{1,0:T(8,128)(2,1)S(1)}, bf16[448,128]{1,0:T(8,128)(2,1)S(1)}, u32[]{:S(2)}, u32[]{:S(2)}) collective-permute-start(bf16[448,128]{1,0:T(8,128)(2,1)S(1)} %get-tuple-element.255), channel_id=1, source_target_pairs={{0,7},{1,6},{2,5},{3,4},{4,3},{5,2},{6,1},{7,0},{8,15},{9,14},{10,... | collective-permute-start | bytes 344072 | tf_op jit(solution)/shard_map/ppermute | solution.py:451
  38.7 8.4 %collective-permute-start.141 = (bf16[448,128]{1,0:T(8,128)(2,1)S(1)}, bf16[448,128]{1,0:T(8,128)(2,1)S(1)}, u32[]{:S(2)}, u32[]{:S(2)}) collective-permute-start(bf16[448,128]{1,0:T(8,128)(2,1)S(1)} %get-tuple-element.256), channel_id=1, source_target_pairs={{0,15},{1,14},{2,13},{3,12},{4,11},{5,10},{6,9},{7,8},{8,7},{9,6},... | collective-permute-start | bytes 344072 | tf_op jit(solution)/shard_map/ppermute | solution.py:451
  50.8 8.3 %collective-permute-start.36 = (bf16[64,1024]{1,0:T(8,128)(2,1)S(1)}, bf16[64,1024]{1,0:T(8,128)(2,1)}, u32[]{:S(2)}, u32[]{:S(2)}) collective-permute-start(bf16[64,1024]{1,0:T(8,128)(2,1)S(1)} %get-tuple-element.379), channel_id=1, source_target_pairs={{0,15},{1,14},{2,13},{3,12},{4,11},{5,10},{6,9},{7,8},{8,7},{9,6},... | collective-permute-start | bytes 393224 | tf_op jit(solution)/shard_map/cond/branch_9_fun/ppermute | solution.py:451
  54.6 9.0 %collective-permute-start.38 = (bf16[64,1024]{1,0:T(8,128)(2,1)S(1)}, bf16[64,1024]{1,0:T(8,128)(2,1)}, u32[]{:S(2)}, u32[]{:S(2)}) collective-permute-start(bf16[64,1024]{1,0:T(8,128)(2,1)S(1)} %get-tuple-element.380), channel_id=1, source_target_pairs={{0,15},{1,14},{2,13},{3,12},{4,11},{5,10},{6,9},{7,8},{8,7},{9,6},... | collective-permute-start | bytes 393224 | tf_op jit(solution)/shard_map/cond/branch_9_fun/ppermute | solution.py:451
  59.2 7.9 %collective-permute-start.37 = (bf16[64,1024]{1,0:T(8,128)(2,1)}, bf16[64,1024]{1,0:T(8,128)(2,1)}, u32[]{:S(2)}, u32[]{:S(2)}) collective-permute-start(bf16[64,1024]{1,0:T(8,128)(2,1)} %collective-permute-done.36), channel_id=1, source_target_pairs={{0,5},{1,4},{2,7},{3,6},{4,1},{5,0},{6,3},{7,2},{8,13},{9,12},{10,... | collective-permute-start | bytes 393224 | tf_op jit(solution)/shard_map/cond/branch_9_fun/ppermute | solution.py:451
  63.6 6.0 %collective-permute-start.39 = (bf16[64,1024]{1,0:T(8,128)(2,1)}, bf16[64,1024]{1,0:T(8,128)(2,1)}, u32[]{:S(2)}, u32[]{:S(2)}) collective-permute-start(bf16[64,1024]{1,0:T(8,128)(2,1)} %collective-permute-done.38), channel_id=1, source_target_pairs={{0,5},{1,4},{2,7},{3,6},{4,1},{5,0},{6,3},{7,2},{8,13},{9,12},{10,... | collective-permute-start | bytes 393224 | tf_op jit(solution)/shard_map/cond/branch_9_fun/ppermute | solution.py:451

commit v4 on v3

--- a/solution.py
+++ b/solution.py
@@ -327,7 +327,7 @@
 
 
 BLOCK = 32
-PIECE = 32
+PIECE = 16
 
 
 def correlate_kernel(

time: 80.6 us -> 79.9 us (level)
  waiting for transfers between devices: 15.6 us -> 16.9 us
  starting transfers between devices: 43.4 us -> 42.4 us
    ppermute x19, waiting for transfers between devices: 15.6 us -> 16.9 us  [swap(): lax.ppermute(block, 'blk', [(low, low ^ mask) for low in range(count)])]
    ppermute x19, starting transfers between devices: 43.4 us -> 42.4 us  [swap(): lax.ppermute(block, 'blk', [(low, low ^ mask) for low in range(count)])]
where the time goes in v4:
time: 79.9 us; the launch traced here: 80.4 us
  starting transfers between devices  42.4 us (53%)
  waiting for transfers between devices  16.9 us (21%)
  Pallas kernels  15.7 us (20%)
  between operations  2.77 us (3%)
  local copies, waits for them, and re-layouts  2.6 us (3%)
    ppermute x19, starting transfers between devices, swap(): lax.ppermute(block, 'blk', [(low, low ^ mask) for low in range(count)])  42.4 us
    ppermute x19, waiting for transfers between devices, swap(): lax.ppermute(block, 'blk', [(low, low ^ mask) for low in range(count)])  16.9 us
    pallas_call x1, Pallas kernels, correlate(): pl.pallas_call(correlate_kernel, in_specs=[pl.BlockSpec(memory_space=pltp...  10.3 us
    pallas_call x1, Pallas kernels, whiten(): pl.pallas_call(functools.partial(whiten_kernel, capacity, plans, places),...  3.05 us
    pallas_call x1, Pallas kernels, pack(): pl.pallas_call(functools.partial(pack_kernel, owners, capacity, plans), i...  2.33 us
  transfers between devices with their start and end apart: 19, of which 8 were waited for; matrix products, arithmetic and copies ran while one was open for 3% of the time, Pallas kernels for 0%

profile of v4, /device:TPU:0, one launch (start us, length us, event | category | flops | bytes accessed | tf_op | source)
XLA Modules:
  0.0 80.4 jit_solution(11775245198606653913)
XLA Ops:
  0.0 2.3 %pack.3 = (bf16[520,128]{1,0:T(8,128)(2,1)S(1)}, bf16[448,128]{1,0:T(8,128)(2,1)S(1)}, bf16[448,128]{1,0:T(8,128)(2,1)S(1)}, bf16[448,128]{1,0:T(8,128)(2,1)S(1)...) custom-call(s32[1]{0:T(128)} %bitcast.1.me_ref, ...), custom_call_target="tpu_custom_call" | custom-call | tf_op jit(solution)/shard_map/pack/pallas_call | solution.py:174
  2.3 4.1 %collective-permute-start.127 = (bf16[448,128]{1,0:T(8,128)(2,1)S(1)}, bf16[448,128]{1,0:T(8,128)(2,1)S(1)}, u32[]{:S(2)}, u32[]{:S(2)}) collective-permute-start(bf16[448,128]{1,0:T(8,128)(2,1)S(1)} %get-tuple-element.242), channel_id=1, source_target_pairs={{0,8},{1,9},{2,10},{3,11},{4,12},{5,13},{6,14},{7,15},{8,0},{9,1},... | collective-permute-start | bytes 344072 | tf_op jit(solution)/shard_map/ppermute | solution.py:451
  6.4 0.0 collective-permute-start.128
  6.4 0.2 collective-permute-start.129
  6.6 1.8 %collective-permute-start.130 = (bf16[448,128]{1,0:T(8,128)(2,1)S(1)}, bf16[448,128]{1,0:T(8,128)(2,1)S(1)}, u32[]{:S(2)}, u32[]{:S(2)}) collective-permute-start(bf16[448,128]{1,0:T(8,128)(2,1)S(1)} %get-tuple-element.245), channel_id=1, source_target_pairs={{0,2},{1,3},{2,0},{3,1},{4,6},{5,7},{6,4},{7,5},{8,10},{9,11},{10,... | collective-permute-start | bytes 344072 | tf_op jit(solution)/shard_map/ppermute | solution.py:451
  8.4 2.5 %collective-permute-start.131 = (bf16[448,128]{1,0:T(8,128)(2,1)S(1)}, bf16[448,128]{1,0:T(8,128)(2,1)S(1)}, u32[]{:S(2)}, u32[]{:S(2)}) collective-permute-start(bf16[448,128]{1,0:T(8,128)(2,1)S(1)} %get-tuple-element.246), channel_id=1, source_target_pairs={{0,10},{1,11},{2,8},{3,9},{4,14},{5,15},{6,12},{7,13},{8,2},{9,3},... | collective-permute-start | bytes 344072 | tf_op jit(solution)/shard_map/ppermute | solution.py:451
  10.9 6.8 %collective-permute-done.127.refs_0_ = bf16[448,128]{1,0:T(8,128)(2,1)S(1)} collective-permute-done((bf16[448,128]{1,0:T(8,128)(2,1)S(1)}, bf16[448,128]{1,0:T(8,128)(2,1)S(1)}, u32[]{:S(2)}, u32[]{:S(2)}) %collective-permute-start.127) | collective-permute-done | bytes 114720 | tf_op jit(solution)/shard_map/ppermute | solution.py:451
  17.8 0.0 collective-permute-start.132
  17.8 0.0 collective-permute-done.128.refs_1_
  17.8 0.7 collective-permute-start.133
  18.5 0.1 collective-permute-done.129.refs_2_
  18.6 3.8 %collective-permute-start.134 = (bf16[448,128]{1,0:T(8,128)(2,1)S(1)}, bf16[448,128]{1,0:T(8,128)(2,1)S(1)}, u32[]{:S(2)}, u32[]{:S(2)}) collective-permute-start(bf16[448,128]{1,0:T(8,128)(2,1)S(1)} %get-tuple-element.249), channel_id=1, source_target_pairs={{0,4},{1,5},{2,6},{3,7},{4,0},{5,1},{6,2},{7,3},{8,12},{9,13},{10,... | collective-permute-start | bytes 344072 | tf_op jit(solution)/shard_map/ppermute | solution.py:451
  22.3 0.0 collective-permute-done.130.refs_3_
  22.3 1.0 %collective-permute-start.135 = (bf16[448,128]{1,0:T(8,128)(2,1)S(1)}, bf16[448,128]{1,0:T(8,128)(2,1)S(1)}, u32[]{:S(2)}, u32[]{:S(2)}) collective-permute-start(bf16[448,128]{1,0:T(8,128)(2,1)S(1)} %get-tuple-element.250), channel_id=1, source_target_pairs={{0,12},{1,13},{2,14},{3,15},{4,8},{5,9},{6,10},{7,11},{8,4},{9,5},... | collective-permute-start | bytes 344072 | tf_op jit(solution)/shard_map/ppermute | solution.py:451
  23.3 0.0 collective-permute-done.131.refs_4_
  23.4 1.4 %collective-permute-start.136 = (bf16[448,128]{1,0:T(8,128)(2,1)S(1)}, bf16[448,128]{1,0:T(8,128)(2,1)S(1)}, u32[]{:S(2)}, u32[]{:S(2)}) collective-permute-start(bf16[448,128]{1,0:T(8,128)(2,1)S(1)} %get-tuple-element.251), channel_id=1, source_target_pairs={{0,5},{1,4},{2,7},{3,6},{4,1},{5,0},{6,3},{7,2},{8,13},{9,12},{10,... | collective-permute-start | bytes 344072 | tf_op jit(solution)/shard_map/ppermute | solution.py:451
  24.7 0.3 collective-permute-done.132.refs_5_
  25.0 3.5 %collective-permute-start.137 = (bf16[448,128]{1,0:T(8,128)(2,1)S(1)}, bf16[448,128]{1,0:T(8,128)(2,1)S(1)}, u32[]{:S(2)}, u32[]{:S(2)}) collective-permute-start(bf16[448,128]{1,0:T(8,128)(2,1)S(1)} %get-tuple-element.252), channel_id=1, source_target_pairs={{0,13},{1,12},{2,15},{3,14},{4,9},{5,8},{6,11},{7,10},{8,5},{9,4},... | collective-permute-start | bytes 344072 | tf_op jit(solution)/shard_map/ppermute | solution.py:451
  28.5 0.0 collective-permute-done.133.refs_6_
  28.5 2.5 %collective-permute-start.138 = (bf16[448,128]{1,0:T(8,128)(2,1)S(1)}, bf16[448,128]{1,0:T(8,128)(2,1)S(1)}, u32[]{:S(2)}, u32[]{:S(2)}) collective-permute-start(bf16[448,128]{1,0:T(8,128)(2,1)S(1)} %get-tuple-element.253), channel_id=1, source_target_pairs={{0,6},{1,7},{2,4},{3,5},{4,2},{5,3},{6,0},{7,1},{8,14},{9,15},{10,... | collective-permute-start | bytes 344072 | tf_op jit(solution)/shard_map/ppermute | solution.py:451
  31.0 0.0 collective-permute-done.134.refs_7_
  31.0 7.7 %collective-permute-start.139 = (bf16[448,128]{1,0:T(8,128)(2,1)S(1)}, bf16[448,128]{1,0:T(8,128)(2,1)S(1)}, u32[]{:S(2)}, u32[]{:S(2)}) collective-permute-start(bf16[448,128]{1,0:T(8,128)(2,1)S(1)} %get-tuple-element.254), channel_id=1, source_target_pairs={{0,14},{1,15},{2,12},{3,13},{4,10},{5,11},{6,8},{7,9},{8,6},{9,7},... | collective-permute-start | bytes 344072 | tf_op jit(solution)/shard_map/ppermute | solution.py:451
  38.7 0.0 collective-permute-done.135.refs_8_
  38.7 0.0 collective-permute-start.140
  38.7 0.0 collective-permute-done.136.refs_9_
  38.7 3.4 %collective-permute-start.141 = (bf16[448,128]{1,0:T(8,128)(2,1)S(1)}, bf16[448,128]{1,0:T(8,128)(2,1)S(1)}, u32[]{:S(2)}, u32[]{:S(2)}) collective-permute-start(bf16[448,128]{1,0:T(8,128)(2,1)S(1)} %get-tuple-element.256), channel_id=1, source_target_pairs={{0,15},{1,14},{2,13},{3,12},{4,11},{5,10},{6,9},{7,8},{8,7},{9,6},... | collective-permute-start | bytes 344072 | tf_op jit(solution)/shard_map/ppermute | solution.py:451
  42.1 1.3 %fusion = (s32[1]{0:T(128)}, s32[1]{0:T(128)}) fusion(s32[2]{0:T(128)} %param.42), kind=kLoop, calls=%fused_computation | loop fusion | bytes 16 | tf_op jit(solution)/shard_map/slice | solution.py:497
  45.3 0.0 collective-permute-done.137.refs_10_
  45.3 0.0 collective-permute-done.138.refs_11_
  45.3 0.0 collective-permute-done.139.refs_12_
  45.3 0.2 collective-permute-done.140.refs_13_
  45.5 1.6 %collective-permute-done.141.refs_14_ = bf16[448,128]{1,0:T(8,128)(2,1)S(1)} collective-permute-done((bf16[448,128]{1,0:T(8,128)(2,1)S(1)}, bf16[448,128]{1,0:T(8,128)(2,1)S(1)}, u32[]{:S(2)}, u32[]{:S(2)}) %collective-permute-start.141) | collective-permute-done | bytes 114720 | tf_op jit(solution)/shard_map/ppermute | solution.py:451
  47.1 3.1 %whiten.3 = (bf16[64,1024]{1,0:T(8,128)(2,1)S(1)}, bf16[64,1024]{1,0:T(8,128)(2,1)S(1)}, s32[1]{0:T(128)}) custom-call(s32[1]{0:T(128)} %bitcast.1.me_ref, s32[1]{0:T(128)} %sub.3.mask_ref, bf16[448,128]{1,0:T(8,128)(2,1)S(1)} %collective-permute-done.127.refs_0_, bf16[448,128]{1,0:T(8,128)(2,1)S(1)} %collective-permute-done.128.refs_1_, ...), custom_call_target="tpu_custom_call" | custom-call | tf_op jit(solution)/shard_map/whiten/pallas_call | solution.py:307
  50.8 19.1 %conditional.2 = (bf16[64,1024]{1,0:T(8,128)(2,1)}, bf16[64,1024]{1,0:T(8,128)(2,1)}, bf16[64,1024]{1,0:T(8,128)(2,1)}, bf16[64,1024]{1,0:T(8,128)(2,1)}, bf16[6...) conditional(s32[]{:T(128)} %bitcast.5, (bf16[64,1024]{1,0:T(8,128)(2,1)S(1)}, ...), branch_computations={%region_0.0_spmd, %region_1.0_spmd, %region_2.0_spmd, %region_3.0_... | conditional | flops 1 | bytes 10085224 | solution.py:507
  50.8 3.8 %collective-permute-start.40 = (bf16[64,1024]{1,0:T(8,128)(2,1)S(1)}, bf16[64,1024]{1,0:T(8,128)(2,1)}, u32[]{:S(2)}, u32[]{:S(2)}) collective-permute-start(bf16[64,1024]{1,0:T(8,128)(2,1)S(1)} %get-tuple-element.385), channel_id=1, source_target_pairs={{0,15},{1,14},{2,13},{3,12},{4,11},{5,10},{6,9},{7,8},{8,7},{9,6},... | collective-permute-start | bytes 393224 | tf_op jit(solution)/shard_map/cond/branch_10_fun/ppermute | solution.py:451
  54.6 0.8 collective-permute-start.42
  55.4 3.8 %collective-permute-done.40 = bf16[64,1024]{1,0:T(8,128)(2,1)} collective-permute-done((bf16[64,1024]{1,0:T(8,128)(2,1)S(1)}, bf16[64,1024]{1,0:T(8,128)(2,1)}, u32[]{:S(2)}, u32[]{:S(2)}) %collective-permute-start.40) | collective-permute-done | bytes 131104 | tf_op jit(solution)/shard_map/cond/branch_10_fun/ppermute | solution.py:451
  59.2 3.2 %collective-permute-start.41 = (bf16[64,1024]{1,0:T(8,128)(2,1)}, bf16[64,1024]{1,0:T(8,128)(2,1)}, u32[]{:S(2)}, u32[]{:S(2)}) collective-permute-start(bf16[64,1024]{1,0:T(8,128)(2,1)} %collective-permute-done.40), channel_id=1, source_target_pairs={{0,4},{1,5},{2,6},{3,7},{4,0},{5,1},{6,2},{7,3},{8,12},{9,13},{10,... | collective-permute-start | bytes 393224 | tf_op jit(solution)/shard_map/cond/branch_10_fun/ppermute | solution.py:451
  62.4 0.9 %collective-permute-done.42 = bf16[64,1024]{1,0:T(8,128)(2,1)} collective-permute-done((bf16[64,1024]{1,0:T(8,128)(2,1)S(1)}, bf16[64,1024]{1,0:T(8,128)(2,1)}, u32[]{:S(2)}, u32[]{:S(2)}) %collective-permute-start.42) | collective-permute-done | bytes 131104 | tf_op jit(solution)/shard_map/cond/branch_10_fun/ppermute | solution.py:451
  63.3 2.1 %collective-permute-start.43 = (bf16[64,1024]{1,0:T(8,128)(2,1)}, bf16[64,1024]{1,0:T(8,128)(2,1)}, u32[]{:S(2)}, u32[]{:S(2)}) collective-permute-start(bf16[64,1024]{1,0:T(8,128)(2,1)} %collective-permute-done.42), channel_id=1, source_target_pairs={{0,4},{1,5},{2,6},{3,7},{4,0},{5,1},{6,2},{7,3},{8,12},{9,13},{10,... | collective-permute-start | bytes 393224 | tf_op jit(solution)/shard_map/cond/branch_10_fun/ppermute | solution.py:451
  65.4 0.7 copy.126
  66.1 0.6 copy.127
  66.7 0.0 collective-permute-done.41
  66.7 3.2 %collective-permute-done.43 = bf16[64,1024]{1,0:T(8,128)(2,1)} collective-permute-done((bf16[64,1024]{1,0:T(8,128)(2,1)}, bf16[64,1024]{1,0:T(8,128)(2,1)}, u32[]{:S(2)}, u32[]{:S(2)}) %collective-permute-start.43) | collective-permute-done | bytes 131104 | tf_op jit(solution)/shard_map/cond/branch_10_fun/ppermute | solution.py:451
  69.9 10.3 %correlate.1 = bf16[2,128,128,128]{3,2,1,0:T(8,128)(2,1)} custom-call(s32[1]{0:T(128)S(6)} %convert_element_type.3.order_ref, bf16[64,1024]{1,0:T(8,128)(2,1)} %get-tuple-element.261.own_low, bf16[64,1024]{1,0:T(8,128)(2,1)} %get-tuple-element.262.own_high, bf16[96,256]{1,0:T(8,128)(2,1)} %constant.29.clone.rows_ref, ...), custom_call_target="tpu_custom_call" | custom-call | tf_op jit(solution)/shard_map/correlate/pallas_call | solution.py:425
Async XLA Ops:
  2.3 15.4 %collective-permute-start.127 = (bf16[448,128]{1,0:T(8,128)(2,1)S(1)}, bf16[448,128]{1,0:T(8,128)(2,1)S(1)}, u32[]{:S(2)}, u32[]{:S(2)}) collective-permute-start(bf16[448,128]{1,0:T(8,128)(2,1)S(1)} %get-tuple-element.242), channel_id=1, source_target_pairs={{0,8},{1,9},{2,10},{3,11},{4,12},{5,13},{6,14},{7,15},{8,0},{9,1},... | collective-permute-start | bytes 344072 | tf_op jit(solution)/shard_map/ppermute | solution.py:451
  6.4 11.4 %collective-permute-start.128 = (bf16[448,128]{1,0:T(8,128)(2,1)S(1)}, bf16[448,128]{1,0:T(8,128)(2,1)S(1)}, u32[]{:S(2)}, u32[]{:S(2)}) collective-permute-start(bf16[448,128]{1,0:T(8,128)(2,1)S(1)} %get-tuple-element.243), channel_id=1, source_target_pairs={{0,1},{1,0},{2,3},{3,2},{4,5},{5,4},{6,7},{7,6},{8,9},{9,8},{10,11... | collective-permute-start | bytes 344072 | tf_op jit(solution)/shard_map/ppermute | solution.py:451
  6.4 12.2 %collective-permute-start.129 = (bf16[448,128]{1,0:T(8,128)(2,1)S(1)}, bf16[448,128]{1,0:T(8,128)(2,1)S(1)}, u32[]{:S(2)}, u32[]{:S(2)}) collective-permute-start(bf16[448,128]{1,0:T(8,128)(2,1)S(1)} %get-tuple-element.244), channel_id=1, source_target_pairs={{0,9},{1,8},{2,11},{3,10},{4,13},{5,12},{6,15},{7,14},{8,1},{9,0},... | collective-permute-start | bytes 344072 | tf_op jit(solution)/shard_map/ppermute | solution.py:451
  6.6 15.7 %collective-permute-start.130 = (bf16[448,128]{1,0:T(8,128)(2,1)S(1)}, bf16[448,128]{1,0:T(8,128)(2,1)S(1)}, u32[]{:S(2)}, u32[]{:S(2)}) collective-permute-start(bf16[448,128]{1,0:T(8,128)(2,1)S(1)} %get-tuple-element.245), channel_id=1, source_target_pairs={{0,2},{1,3},{2,0},{3,1},{4,6},{5,7},{6,4},{7,5},{8,10},{9,11},{10,... | collective-permute-start | bytes 344072 | tf_op jit(solution)/shard_map/ppermute | solution.py:451
  8.4 14.9 %collective-permute-start.131 = (bf16[448,128]{1,0:T(8,128)(2,1)S(1)}, bf16[448,128]{1,0:T(8,128)(2,1)S(1)}, u32[]{:S(2)}, u32[]{:S(2)}) collective-permute-start(bf16[448,128]{1,0:T(8,128)(2,1)S(1)} %get-tuple-element.246), channel_id=1, source_target_pairs={{0,10},{1,11},{2,8},{3,9},{4,14},{5,15},{6,12},{7,13},{8,2},{9,3},... | collective-permute-start | bytes 344072 | tf_op jit(solution)/shard_map/ppermute | solution.py:451
  17.8 7.2 %collective-permute-start.132 = (bf16[448,128]{1,0:T(8,128)(2,1)S(1)}, bf16[448,128]{1,0:T(8,128)(2,1)S(1)}, u32[]{:S(2)}, u32[]{:S(2)}) collective-permute-start(bf16[448,128]{1,0:T(8,128)(2,1)S(1)} %get-tuple-element.247), channel_id=1, source_target_pairs={{0,3},{1,2},{2,1},{3,0},{4,7},{5,6},{6,5},{7,4},{8,11},{9,10},{10,... | collective-permute-start | bytes 344072 | tf_op jit(solution)/shard_map/ppermute | solution.py:451
  17.8 10.7 %collective-permute-start.133 = (bf16[448,128]{1,0:T(8,128)(2,1)S(1)}, bf16[448,128]{1,0:T(8,128)(2,1)S(1)}, u32[]{:S(2)}, u32[]{:S(2)}) collective-permute-start(bf16[448,128]{1,0:T(8,128)(2,1)S(1)} %get-tuple-element.248), channel_id=1, source_target_pairs={{0,11},{1,10},{2,9},{3,8},{4,15},{5,14},{6,13},{7,12},{8,3},{9,2},... | collective-permute-start | bytes 344072 | tf_op jit(solution)/shard_map/ppermute | solution.py:451
  18.6 12.4 %collective-permute-start.134 = (bf16[448,128]{1,0:T(8,128)(2,1)S(1)}, bf16[448,128]{1,0:T(8,128)(2,1)S(1)}, u32[]{:S(2)}, u32[]{:S(2)}) collective-permute-start(bf16[448,128]{1,0:T(8,128)(2,1)S(1)} %get-tuple-element.249), channel_id=1, source_target_pairs={{0,4},{1,5},{2,6},{3,7},{4,0},{5,1},{6,2},{7,3},{8,12},{9,13},{10,... | collective-permute-start | bytes 344072 | tf_op jit(solution)/shard_map/ppermute | solution.py:451
  22.3 16.4 %collective-permute-start.135 = (bf16[448,128]{1,0:T(8,128)(2,1)S(1)}, bf16[448,128]{1,0:T(8,128)(2,1)S(1)}, u32[]{:S(2)}, u32[]{:S(2)}) collective-permute-start(bf16[448,128]{1,0:T(8,128)(2,1)S(1)} %get-tuple-element.250), channel_id=1, source_target_pairs={{0,12},{1,13},{2,14},{3,15},{4,8},{5,9},{6,10},{7,11},{8,4},{9,5},... | collective-permute-start | bytes 344072 | tf_op jit(solution)/shard_map/ppermute | solution.py:451
  23.4 15.3 %collective-permute-start.136 = (bf16[448,128]{1,0:T(8,128)(2,1)S(1)}, bf16[448,128]{1,0:T(8,128)(2,1)S(1)}, u32[]{:S(2)}, u32[]{:S(2)}) collective-permute-start(bf16[448,128]{1,0:T(8,128)(2,1)S(1)} %get-tuple-element.251), channel_id=1, source_target_pairs={{0,5},{1,4},{2,7},{3,6},{4,1},{5,0},{6,3},{7,2},{8,13},{9,12},{10,... | collective-permute-start | bytes 344072 | tf_op jit(solution)/shard_map/ppermute | solution.py:451
  25.0 20.3 %collective-permute-start.137 = (bf16[448,128]{1,0:T(8,128)(2,1)S(1)}, bf16[448,128]{1,0:T(8,128)(2,1)S(1)}, u32[]{:S(2)}, u32[]{:S(2)}) collective-permute-start(bf16[448,128]{1,0:T(8,128)(2,1)S(1)} %get-tuple-element.252), channel_id=1, source_target_pairs={{0,13},{1,12},{2,15},{3,14},{4,9},{5,8},{6,11},{7,10},{8,5},{9,4},... | collective-permute-start | bytes 344072 | tf_op jit(solution)/shard_map/ppermute | solution.py:451
  28.5 16.9 %collective-permute-start.138 = (bf16[448,128]{1,0:T(8,128)(2,1)S(1)}, bf16[448,128]{1,0:T(8,128)(2,1)S(1)}, u32[]{:S(2)}, u32[]{:S(2)}) collective-permute-start(bf16[448,128]{1,0:T(8,128)(2,1)S(1)} %get-tuple-element.253), channel_id=1, source_target_pairs={{0,6},{1,7},{2,4},{3,5},{4,2},{5,3},{6,0},{7,1},{8,14},{9,15},{10,... | collective-permute-start | bytes 344072 | tf_op jit(solution)/shard_map/ppermute | solution.py:451
  31.0 14.4 %collective-permute-start.139 = (bf16[448,128]{1,0:T(8,128)(2,1)S(1)}, bf16[448,128]{1,0:T(8,128)(2,1)S(1)}, u32[]{:S(2)}, u32[]{:S(2)}) collective-permute-start(bf16[448,128]{1,0:T(8,128)(2,1)S(1)} %get-tuple-element.254), channel_id=1, source_target_pairs={{0,14},{1,15},{2,12},{3,13},{4,10},{5,11},{6,8},{7,9},{8,6},{9,7},... | collective-permute-start | bytes 344072 | tf_op jit(solution)/shard_map/ppermute | solution.py:451
  38.7 6.8 %collective-permute-start.140 = (bf16[448,128]{1,0:T(8,128)(2,1)S(1)}, bf16[448,128]{1,0:T(8,128)(2,1)S(1)}, u32[]{:S(2)}, u32[]{:S(2)}) collective-permute-start(bf16[448,128]{1,0:T(8,128)(2,1)S(1)} %get-tuple-element.255), channel_id=1, source_target_pairs={{0,7},{1,6},{2,5},{3,4},{4,3},{5,2},{6,1},{7,0},{8,15},{9,14},{10,... | collective-permute-start | bytes 344072 | tf_op jit(solution)/shard_map/ppermute | solution.py:451
  38.7 8.4 %collective-permute-start.141 = (bf16[448,128]{1,0:T(8,128)(2,1)S(1)}, bf16[448,128]{1,0:T(8,128)(2,1)S(1)}, u32[]{:S(2)}, u32[]{:S(2)}) collective-permute-start(bf16[448,128]{1,0:T(8,128)(2,1)S(1)} %get-tuple-element.256), channel_id=1, source_target_pairs={{0,15},{1,14},{2,13},{3,12},{4,11},{5,10},{6,9},{7,8},{8,7},{9,6},... | collective-permute-start | bytes 344072 | tf_op jit(solution)/shard_map/ppermute | solution.py:451
  50.8 8.3 %collective-permute-start.40 = (bf16[64,1024]{1,0:T(8,128)(2,1)S(1)}, bf16[64,1024]{1,0:T(8,128)(2,1)}, u32[]{:S(2)}, u32[]{:S(2)}) collective-permute-start(bf16[64,1024]{1,0:T(8,128)(2,1)S(1)} %get-tuple-element.385), channel_id=1, source_target_pairs={{0,15},{1,14},{2,13},{3,12},{4,11},{5,10},{6,9},{7,8},{8,7},{9,6},... | collective-permute-start | bytes 393224 | tf_op jit(solution)/shard_map/cond/branch_10_fun/ppermute | solution.py:451
  54.6 8.7 %collective-permute-start.42 = (bf16[64,1024]{1,0:T(8,128)(2,1)S(1)}, bf16[64,1024]{1,0:T(8,128)(2,1)}, u32[]{:S(2)}, u32[]{:S(2)}) collective-permute-start(bf16[64,1024]{1,0:T(8,128)(2,1)S(1)} %get-tuple-element.386), channel_id=1, source_target_pairs={{0,15},{1,14},{2,13},{3,12},{4,11},{5,10},{6,9},{7,8},{8,7},{9,6},... | collective-permute-start | bytes 393224 | tf_op jit(solution)/shard_map/cond/branch_10_fun/ppermute | solution.py:451
  59.2 7.5 %collective-permute-start.41 = (bf16[64,1024]{1,0:T(8,128)(2,1)}, bf16[64,1024]{1,0:T(8,128)(2,1)}, u32[]{:S(2)}, u32[]{:S(2)}) collective-permute-start(bf16[64,1024]{1,0:T(8,128)(2,1)} %collective-permute-done.40), channel_id=1, source_target_pairs={{0,4},{1,5},{2,6},{3,7},{4,0},{5,1},{6,2},{7,3},{8,12},{9,13},{10,... | collective-permute-start | bytes 393224 | tf_op jit(solution)/shard_map/cond/branch_10_fun/ppermute | solution.py:451
  63.3 6.6 %collective-permute-start.43 = (bf16[64,1024]{1,0:T(8,128)(2,1)}, bf16[64,1024]{1,0:T(8,128)(2,1)}, u32[]{:S(2)}, u32[]{:S(2)}) collective-permute-start(bf16[64,1024]{1,0:T(8,128)(2,1)} %collective-permute-done.42), channel_id=1, source_target_pairs={{0,4},{1,5},{2,6},{3,7},{4,0},{5,1},{6,2},{7,3},{8,12},{9,13},{10,... | collective-permute-start | bytes 393224 | tf_op jit(solution)/shard_map/cond/branch_10_fun/ppermute | solution.py:451
